TPU v7x, 128 devices: a whole 4x4x4 slice. The times are simulated.
128 devices in a mesh: qa: 16 (over y, x), kb: 8 (over z, core).
Axes of the slice: x: 4, y: 4, z: 4, core: 2. Of those that a mesh axis runs over, the one named last changes fastest.
Arguments:
- query_rows: bfloat16 [79872, 128], P(('qa', 'kb')), may hold values from -240 to 240
- key_rows: bfloat16 [79872, 128], P(('qa', 'kb')), may hold values from -7 to 7
- value_rows: bfloat16 [79872, 128], P(('qa', 'kb')), may hold values from -6 to 6
- pair_table: int32 [16, 16], replicated, may hold values from 0 to 1, as said below
- frame_offset: int32 [16], replicated, may hold values from 0 to 47
- height_offset: int32 [16], replicated, may hold values from 0 to 15
- width_offset: int32 [16], replicated, may hold values from 0 to 15
Outputs:
- attended: bfloat16 [79872, 128], P(('qa', 'kb'))
Inputs may be any that keep to these rules, and one draw needn't show every extreme that they name: pair_table[c][c] is 1, pair_table[c][d] is 0 for d > c, and entries below the diagonal are 0 or 1.
All inputs are finite; a program needn't handle non-finite values.
Results may differ from a plain program's by a relative error of at most 0.017.
Values may be sent and summed in bfloat16 or wider, within the bound.
A program may use at most 64 MiB of HBM per device.

v0:
```python
import jax
import jax.numpy as jnp
from jax import lax
from jax.sharding import PartitionSpec as P

HEIGHT = 32
WIDTH = 52


NEGATIVE = -1e30


def angle_table(frame_pos, height_pos, width_pos, head_size):
    pair_count = head_size // 2
    side_count = pair_count // 3
    lead_count = pair_count - 2 * side_count

    def frequency(number):
        return 1.0 / 10000.0 ** (jnp.arange(number, dtype=jnp.float32) / number)

    return jnp.concatenate(
        [
            frame_pos.astype(jnp.float32)[:, None] * frequency(lead_count)[None, :],
            height_pos.astype(jnp.float32)[:, None] * frequency(side_count)[None, :],
            width_pos.astype(jnp.float32)[:, None] * frequency(side_count)[None, :],
        ],
        axis=1,
    )


def rotate(rows_in, angles):
    half_cols = rows_in.shape[1] // 2
    leading = rows_in[:, :half_cols].astype(jnp.float32)
    trailing = rows_in[:, half_cols:].astype(jnp.float32)
    cosine = jnp.cos(angles)
    sine = jnp.sin(angles)
    return jnp.concatenate(
        [leading * cosine - trailing * sine, leading * sine + trailing * cosine], axis=1
    ).astype(jnp.bfloat16)


def update_group(current, query_block, key_block, value_block, score_scale):
    maxima, totals, numerators = current
    scores = (
        lax.dot_general(
            query_block, key_block, (((1,), (1,)), ((), ())), preferred_element_type=jnp.float32
        )
        * score_scale
    )
    new_max = jnp.maximum(maxima, jnp.max(scores, axis=1))
    shrink = jnp.exp(maxima - new_max)
    weights = jnp.exp(scores - new_max[:, None])
    totals = totals * shrink + jnp.sum(weights, axis=1)
    numerators = numerators * shrink[:, None] + jnp.dot(
        weights.astype(jnp.bfloat16), value_block, preferred_element_type=jnp.float32
    )
    return (new_max, totals, numerators)


def attend(running, query_groups, query_spans, key_groups, value_groups, key_spans, pair_table):
    key_count = key_groups.shape[0]
    score_scale = float(query_groups.shape[2]) ** (-0.5)

    def visit(running, query_index, key_index):
        allowed = pair_table[query_spans[query_index], key_spans[key_index]] > 0
        current = (running[0][query_index], running[1][query_index], running[2][query_index])
        updated = lax.cond(
            allowed,
            lambda present: update_group(
                present,
                query_groups[query_index],
                key_groups[key_index],
                value_groups[key_index],
                score_scale,
            ),
            lambda present: present,
            current,
        )
        return (
            running[0].at[query_index].set(updated[0]),
            running[1].at[query_index].set(updated[1]),
            running[2].at[query_index].set(updated[2]),
        )

    def over_keys(key_index, running):
        running = visit(running, 0, key_index)
        return running

    return lax.fori_loop(0, key_count, over_keys, running)


def start_state(group_count, group_rows, head_size):
    return (
        jnp.full((group_count, group_rows), NEGATIVE, jnp.float32),
        jnp.zeros((group_count, group_rows), jnp.float32),
        jnp.zeros((group_count, group_rows, head_size), jnp.float32),
    )


def combine_sources(received):
    maxima, totals, numerators = received
    largest = jnp.max(maxima, axis=0)
    weight = jnp.exp(maxima - largest[None])
    total_sum = jnp.sum(weight * totals, axis=0)
    numerator_sum = jnp.sum(weight[..., None] * numerators, axis=0)
    return (numerator_sum / total_sum[:, None]).astype(jnp.bfloat16)


def local(query_rows, key_rows, value_rows, pair_table, frame_offset, height_offset, width_offset):
    tile_rows, head_size = query_rows.shape
    span_id = lax.axis_index("qa")
    tile_index = lax.axis_index("kb")
    column_devices = lax.axis_size("kb")
    within = tile_index * tile_rows + jnp.arange(tile_rows, dtype=jnp.int32)
    frame_pos = within // (HEIGHT * WIDTH) + lax.dynamic_index_in_dim(
        frame_offset, span_id, keepdims=False
    )
    height_pos = within // WIDTH % HEIGHT + lax.dynamic_index_in_dim(
        height_offset, span_id, keepdims=False
    )
    width_pos = within % WIDTH + lax.dynamic_index_in_dim(width_offset, span_id, keepdims=False)
    angles = angle_table(frame_pos, height_pos, width_pos, head_size)
    query_turned = rotate(query_rows, angles)
    key_turned = rotate(key_rows, angles)
    row_queries = lax.all_gather(query_turned, "kb", axis=0, tiled=True)
    query_groups = row_queries[None]
    query_spans = jnp.reshape(span_id, (1,))
    initial = start_state(query_groups.shape[0], query_groups.shape[1], head_size)
    key_piece = lax.all_gather(key_turned, "qa", axis=0, tiled=True)
    value_piece = lax.all_gather(value_rows, "qa", axis=0, tiled=True)
    piece_tiles = key_piece.shape[0] // tile_rows
    key_groups = key_piece.reshape(piece_tiles, tile_rows, head_size)
    value_groups = value_piece.reshape(piece_tiles, tile_rows, head_size)
    key_spans = jnp.arange(piece_tiles, dtype=jnp.int32)
    maxima, totals, numerators = attend(
        initial, query_groups, query_spans, key_groups, value_groups, key_spans, pair_table
    )
    maxima = maxima[0]
    totals = totals[0]
    numerators = numerators[0]
    received = (
        lax.all_to_all(
            maxima.reshape(column_devices, tile_rows), "kb", split_axis=0, concat_axis=0, tiled=True
        ),
        lax.all_to_all(
            totals.reshape(column_devices, tile_rows), "kb", split_axis=0, concat_axis=0, tiled=True
        ),
        lax.all_to_all(
            numerators.reshape(column_devices, tile_rows, head_size),
            "kb",
            split_axis=0,
            concat_axis=0,
            tiled=True,
        ),
    )
    return combine_sources(received)


def solution(mesh):
    in_specs = (
        P(("qa", "kb"), None),
        P(("qa", "kb"), None),
        P(("qa", "kb"), None),
        P(),
        P(),
        P(),
        P(),
    )
    out_specs = P(("qa", "kb"), None)
    return jax.shard_map(local, mesh=mesh, in_specs=in_specs, out_specs=out_specs, check_vma=False)
```

profile of v0, /device:TPU:24, one launch (start us, length us, event | category | flops | bytes accessed | tf_op | source)
XLA Modules:
  0.0 377.8 jit_solution(14569550634847332284)
XLA Ops:
  7.8 1.3 dynamic_slice.39
  13.7 1.4 fusion.33
  18.4 24.8 %all-gather.6.cloned.1.call-done = bf16[4992,128]{1,0:T(8,128)(2,1)} async-done(((bf16[624,128]{1,0:T(8,128)(2,1)}), bf16[4992,128]{1,0:T(8,128)(2,1)}) %all-gather.6.cloned.1.call-update) | async-done | bytes 1277968 | tf_op jit(solution)/shard_map/all_gather | solution.py:125
  43.3 47.8 %all-gather.4.cloned.1.call-done = bf16[9984,128]{1,0:T(8,128)(2,1)} async-done(((bf16[624,128]{1,0:T(8,128)(2,1)}), bf16[9984,128]{1,0:T(8,128)(2,1)}) %all-gather.4.cloned.1.call-update) | async-done | bytes 2555920 | tf_op jit(solution)/shard_map/all_gather | solution.py:129
  91.0 47.7 %all-gather.8.cloned.1.call-done = bf16[9984,128]{1,0:T(8,128)(2,1)} async-done(((bf16[624,128]{1,0:T(8,128)(2,1)}), bf16[9984,128]{1,0:T(8,128)(2,1)}) %all-gather.8.cloned.1.call-update) | async-done | bytes 2555920 | tf_op jit(solution)/shard_map/all_gather | solution.py:130
  138.7 1.7 broadcast_in_dim.8
  140.4 175.2 %while.23 = (s32[]{:T(128)}, f32[1,4992]{1,0:T(1,128)S(1)}, f32[1,4992]{1,0:T(1,128)S(1)}, f32[1,4992,128]{2,1,0:T(8,128)}, s32[16]{0:T(128)S(1)}, /*index=5*/s3...) while((s32[]{:T(128)}, f32[1,4992]{1,0:T(1,128)S(1)}, ...), condition=%wide.region_5.6_spmd, body=%wide.region_0.5_spmd.sunk | while | flops 1621092096 | bytes 44568940 | solution.py:89
  143.0 1.3 dynamic_slice.54
  145.0 11.2 %conditional.2 = (f32[1,4992,128]{2,1,0:T(8,128)}, f32[4992]{0:T(1024)S(1)}, f32[4992]{0:T(1024)S(1)}) conditional(s32[]{:T(128)} %bitcast.34, (f32[4992]{0:T(1024)S(1)}, f32[4992]{0:T(1024)S(1)}, f32[4992,128]{1,0:T(8,128)}) %tuple.119, (s32[]{:T(128)}, bf16[16,624,128]{2,1,0:T(8,128)(2,1)}, bf16[4992,128]{1,0:T(8,128)(2,1)S(1)}, ...), branch_computations={%region_1.1_spmd, %region_2.4_spmd} | conditional | flops 1621092096 | bytes 44408896 | solution.py:67
  145.0 2.8 multiply_reduce_fusion
  147.8 2.0 fusion.1
  149.9 6.3 %fusion.9 = f32[1,4992,128]{2,1,0:T(8,128)} fusion(f32[624,4992]{1,0:T(8,128)S(1)} %get-tuple-element.469, f32[4992]{0:T(1024)S(1)} %max.2, f32[4992,128]{1,0:T(8,128)} %get-tuple-element.393, f32[4992]{0:T(1024)S(1)} %get-tuple-element.465, bf16[16,624,128]{2,1,0:T(8,128)(2,1)} %get-tuple-element.394, s32[]{:T(128)S(6)} %select_n.65), kind=kOutput, calls=%fused_computation.8 | convolution fusion | flops 808065024 | bytes 17771524 | tf_op jit(solution)/shard_map/while/body/eval_jaxpr/cond/branch_1_fun/dot_general | solution.py:54
  158.8 1.3 dynamic_slice.54
  160.9 11.2 %conditional.2 = (f32[1,4992,128]{2,1,0:T(8,128)}, f32[4992]{0:T(1024)S(1)}, f32[4992]{0:T(1024)S(1)}) conditional(s32[]{:T(128)} %bitcast.34, (f32[4992]{0:T(1024)S(1)}, f32[4992]{0:T(1024)S(1)}, f32[4992,128]{1,0:T(8,128)}) %tuple.119, (s32[]{:T(128)}, bf16[16,624,128]{2,1,0:T(8,128)(2,1)}, bf16[4992,128]{1,0:T(8,128)(2,1)S(1)}, ...), branch_computations={%region_1.1_spmd, %region_2.4_spmd} | conditional | flops 1621092096 | bytes 44408896 | solution.py:67
  160.9 2.8 multiply_reduce_fusion
  163.7 2.0 fusion.1
  165.7 6.3 %fusion.9 = f32[1,4992,128]{2,1,0:T(8,128)} fusion(f32[624,4992]{1,0:T(8,128)S(1)} %get-tuple-element.469, f32[4992]{0:T(1024)S(1)} %max.2, f32[4992,128]{1,0:T(8,128)} %get-tuple-element.393, f32[4992]{0:T(1024)S(1)} %get-tuple-element.465, bf16[16,624,128]{2,1,0:T(8,128)(2,1)} %get-tuple-element.394, s32[]{:T(128)S(6)} %select_n.65), kind=kOutput, calls=%fused_computation.8 | convolution fusion | flops 808065024 | bytes 17771524 | tf_op jit(solution)/shard_map/while/body/eval_jaxpr/cond/branch_1_fun/dot_general | solution.py:54
  174.7 1.3 dynamic_slice.54
  179.3 1.3 dynamic_slice.54
  184.0 1.3 dynamic_slice.54
  186.0 11.2 %conditional.2 = (f32[1,4992,128]{2,1,0:T(8,128)}, f32[4992]{0:T(1024)S(1)}, f32[4992]{0:T(1024)S(1)}) conditional(s32[]{:T(128)} %bitcast.34, (f32[4992]{0:T(1024)S(1)}, f32[4992]{0:T(1024)S(1)}, f32[4992,128]{1,0:T(8,128)}) %tuple.119, (s32[]{:T(128)}, bf16[16,624,128]{2,1,0:T(8,128)(2,1)}, bf16[4992,128]{1,0:T(8,128)(2,1)S(1)}, ...), branch_computations={%region_1.1_spmd, %region_2.4_spmd} | conditional | flops 1621092096 | bytes 44408896 | solution.py:67
  186.0 2.8 multiply_reduce_fusion
  188.8 2.0 fusion.1
  190.9 6.3 %fusion.9 = f32[1,4992,128]{2,1,0:T(8,128)} fusion(f32[624,4992]{1,0:T(8,128)S(1)} %get-tuple-element.469, f32[4992]{0:T(1024)S(1)} %max.2, f32[4992,128]{1,0:T(8,128)} %get-tuple-element.393, f32[4992]{0:T(1024)S(1)} %get-tuple-element.465, bf16[16,624,128]{2,1,0:T(8,128)(2,1)} %get-tuple-element.394, s32[]{:T(128)S(6)} %select_n.65), kind=kOutput, calls=%fused_computation.8 | convolution fusion | flops 808065024 | bytes 17771524 | tf_op jit(solution)/shard_map/while/body/eval_jaxpr/cond/branch_1_fun/dot_general | solution.py:54
  199.8 1.3 dynamic_slice.54
  204.5 1.3 dynamic_slice.54
  206.5 11.2 %conditional.2 = (f32[1,4992,128]{2,1,0:T(8,128)}, f32[4992]{0:T(1024)S(1)}, f32[4992]{0:T(1024)S(1)}) conditional(s32[]{:T(128)} %bitcast.34, (f32[4992]{0:T(1024)S(1)}, f32[4992]{0:T(1024)S(1)}, f32[4992,128]{1,0:T(8,128)}) %tuple.119, (s32[]{:T(128)}, bf16[16,624,128]{2,1,0:T(8,128)(2,1)}, bf16[4992,128]{1,0:T(8,128)(2,1)S(1)}, ...), branch_computations={%region_1.1_spmd, %region_2.4_spmd} | conditional | flops 1621092096 | bytes 44408896 | solution.py:67
  206.6 2.8 multiply_reduce_fusion
  209.3 2.0 fusion.1
  211.4 6.3 %fusion.9 = f32[1,4992,128]{2,1,0:T(8,128)} fusion(f32[624,4992]{1,0:T(8,128)S(1)} %get-tuple-element.469, f32[4992]{0:T(1024)S(1)} %max.2, f32[4992,128]{1,0:T(8,128)} %get-tuple-element.393, f32[4992]{0:T(1024)S(1)} %get-tuple-element.465, bf16[16,624,128]{2,1,0:T(8,128)(2,1)} %get-tuple-element.394, s32[]{:T(128)S(6)} %select_n.65), kind=kOutput, calls=%fused_computation.8 | convolution fusion | flops 808065024 | bytes 17771524 | tf_op jit(solution)/shard_map/while/body/eval_jaxpr/cond/branch_1_fun/dot_general | solution.py:54
  220.3 1.3 dynamic_slice.54
  222.4 11.2 %conditional.2 = (f32[1,4992,128]{2,1,0:T(8,128)}, f32[4992]{0:T(1024)S(1)}, f32[4992]{0:T(1024)S(1)}) conditional(s32[]{:T(128)} %bitcast.34, (f32[4992]{0:T(1024)S(1)}, f32[4992]{0:T(1024)S(1)}, f32[4992,128]{1,0:T(8,128)}) %tuple.119, (s32[]{:T(128)}, bf16[16,624,128]{2,1,0:T(8,128)(2,1)}, bf16[4992,128]{1,0:T(8,128)(2,1)S(1)}, ...), branch_computations={%region_1.1_spmd, %region_2.4_spmd} | conditional | flops 1621092096 | bytes 44408896 | solution.py:67
  222.4 2.8 multiply_reduce_fusion
  225.2 2.0 fusion.1
  227.2 6.3 %fusion.9 = f32[1,4992,128]{2,1,0:T(8,128)} fusion(f32[624,4992]{1,0:T(8,128)S(1)} %get-tuple-element.469, f32[4992]{0:T(1024)S(1)} %max.2, f32[4992,128]{1,0:T(8,128)} %get-tuple-element.393, f32[4992]{0:T(1024)S(1)} %get-tuple-element.465, bf16[16,624,128]{2,1,0:T(8,128)(2,1)} %get-tuple-element.394, s32[]{:T(128)S(6)} %select_n.65), kind=kOutput, calls=%fused_computation.8 | convolution fusion | flops 808065024 | bytes 17771524 | tf_op jit(solution)/shard_map/while/body/eval_jaxpr/cond/branch_1_fun/dot_general | solution.py:54
  236.2 1.3 dynamic_slice.54
  240.8 1.3 dynamic_slice.54
  242.9 11.2 %conditional.2 = (f32[1,4992,128]{2,1,0:T(8,128)}, f32[4992]{0:T(1024)S(1)}, f32[4992]{0:T(1024)S(1)}) conditional(s32[]{:T(128)} %bitcast.34, (f32[4992]{0:T(1024)S(1)}, f32[4992]{0:T(1024)S(1)}, f32[4992,128]{1,0:T(8,128)}) %tuple.119, (s32[]{:T(128)}, bf16[16,624,128]{2,1,0:T(8,128)(2,1)}, bf16[4992,128]{1,0:T(8,128)(2,1)S(1)}, ...), branch_computations={%region_1.1_spmd, %region_2.4_spmd} | conditional | flops 1621092096 | bytes 44408896 | solution.py:67
  242.9 2.8 multiply_reduce_fusion
  245.7 2.0 fusion.1
  247.8 6.3 %fusion.9 = f32[1,4992,128]{2,1,0:T(8,128)} fusion(f32[624,4992]{1,0:T(8,128)S(1)} %get-tuple-element.469, f32[4992]{0:T(1024)S(1)} %max.2, f32[4992,128]{1,0:T(8,128)} %get-tuple-element.393, f32[4992]{0:T(1024)S(1)} %get-tuple-element.465, bf16[16,624,128]{2,1,0:T(8,128)(2,1)} %get-tuple-element.394, s32[]{:T(128)S(6)} %select_n.65), kind=kOutput, calls=%fused_computation.8 | convolution fusion | flops 808065024 | bytes 17771524 | tf_op jit(solution)/shard_map/while/body/eval_jaxpr/cond/branch_1_fun/dot_general | solution.py:54
  256.7 1.3 dynamic_slice.54
  258.7 11.2 %conditional.2 = (f32[1,4992,128]{2,1,0:T(8,128)}, f32[4992]{0:T(1024)S(1)}, f32[4992]{0:T(1024)S(1)}) conditional(s32[]{:T(128)} %bitcast.34, (f32[4992]{0:T(1024)S(1)}, f32[4992]{0:T(1024)S(1)}, f32[4992,128]{1,0:T(8,128)}) %tuple.119, (s32[]{:T(128)}, bf16[16,624,128]{2,1,0:T(8,128)(2,1)}, bf16[4992,128]{1,0:T(8,128)(2,1)S(1)}, ...), branch_computations={%region_1.1_spmd, %region_2.4_spmd} | conditional | flops 1621092096 | bytes 44408896 | solution.py:67
  258.7 2.8 multiply_reduce_fusion
  261.5 2.0 fusion.1
  263.6 6.3 %fusion.9 = f32[1,4992,128]{2,1,0:T(8,128)} fusion(f32[624,4992]{1,0:T(8,128)S(1)} %get-tuple-element.469, f32[4992]{0:T(1024)S(1)} %max.2, f32[4992,128]{1,0:T(8,128)} %get-tuple-element.393, f32[4992]{0:T(1024)S(1)} %get-tuple-element.465, bf16[16,624,128]{2,1,0:T(8,128)(2,1)} %get-tuple-element.394, s32[]{:T(128)S(6)} %select_n.65), kind=kOutput, calls=%fused_computation.8 | convolution fusion | flops 808065024 | bytes 17771524 | tf_op jit(solution)/shard_map/while/body/eval_jaxpr/cond/branch_1_fun/dot_general | solution.py:54
  272.5 1.3 dynamic_slice.54
  274.6 11.2 %conditional.2 = (f32[1,4992,128]{2,1,0:T(8,128)}, f32[4992]{0:T(1024)S(1)}, f32[4992]{0:T(1024)S(1)}) conditional(s32[]{:T(128)} %bitcast.34, (f32[4992]{0:T(1024)S(1)}, f32[4992]{0:T(1024)S(1)}, f32[4992,128]{1,0:T(8,128)}) %tuple.119, (s32[]{:T(128)}, bf16[16,624,128]{2,1,0:T(8,128)(2,1)}, bf16[4992,128]{1,0:T(8,128)(2,1)S(1)}, ...), branch_computations={%region_1.1_spmd, %region_2.4_spmd} | conditional | flops 1621092096 | bytes 44408896 | solution.py:67
  274.6 2.8 multiply_reduce_fusion
  277.4 2.0 fusion.1
  279.4 6.3 %fusion.9 = f32[1,4992,128]{2,1,0:T(8,128)} fusion(f32[624,4992]{1,0:T(8,128)S(1)} %get-tuple-element.469, f32[4992]{0:T(1024)S(1)} %max.2, f32[4992,128]{1,0:T(8,128)} %get-tuple-element.393, f32[4992]{0:T(1024)S(1)} %get-tuple-element.465, bf16[16,624,128]{2,1,0:T(8,128)(2,1)} %get-tuple-element.394, s32[]{:T(128)S(6)} %select_n.65), kind=kOutput, calls=%fused_computation.8 | convolution fusion | flops 808065024 | bytes 17771524 | tf_op jit(solution)/shard_map/while/body/eval_jaxpr/cond/branch_1_fun/dot_general | solution.py:54
  288.4 1.3 dynamic_slice.54
  290.4 11.2 %conditional.2 = (f32[1,4992,128]{2,1,0:T(8,128)}, f32[4992]{0:T(1024)S(1)}, f32[4992]{0:T(1024)S(1)}) conditional(s32[]{:T(128)} %bitcast.34, (f32[4992]{0:T(1024)S(1)}, f32[4992]{0:T(1024)S(1)}, f32[4992,128]{1,0:T(8,128)}) %tuple.119, (s32[]{:T(128)}, bf16[16,624,128]{2,1,0:T(8,128)(2,1)}, bf16[4992,128]{1,0:T(8,128)(2,1)S(1)}, ...), branch_computations={%region_1.1_spmd, %region_2.4_spmd} | conditional | flops 1621092096 | bytes 44408896 | solution.py:67
  290.4 2.8 multiply_reduce_fusion
  293.2 2.0 fusion.1
  295.3 6.3 %fusion.9 = f32[1,4992,128]{2,1,0:T(8,128)} fusion(f32[624,4992]{1,0:T(8,128)S(1)} %get-tuple-element.469, f32[4992]{0:T(1024)S(1)} %max.2, f32[4992,128]{1,0:T(8,128)} %get-tuple-element.393, f32[4992]{0:T(1024)S(1)} %get-tuple-element.465, bf16[16,624,128]{2,1,0:T(8,128)(2,1)} %get-tuple-element.394, s32[]{:T(128)S(6)} %select_n.65), kind=kOutput, calls=%fused_computation.8 | convolution fusion | flops 808065024 | bytes 17771524 | tf_op jit(solution)/shard_map/while/body/eval_jaxpr/cond/branch_1_fun/dot_general | solution.py:54
  304.2 1.3 dynamic_slice.54
  308.9 1.3 dynamic_slice.54
  313.5 1.3 dynamic_slice.54
  316.4 4.4 %all-to-all-start = ((f32[8,1,624]{2,1,0:T(1,128)}), f32[8,1,624]{2,1,0:T(1,128)S(1)}, u32[]{:S(2)}, u32[]{:S(2)}) async-start(f32[8,1,624]{2,1,0:T(1,128)} %all_to_all.19), calls=%async_computation | async-start | bytes 40960 | tf_op jit(solution)/shard_map/all_to_all | solution.py:142
  321.0 5.2 %all-to-all-done = f32[8,1,624]{2,1,0:T(1,128)S(1)} async-done(((f32[8,1,624]{2,1,0:T(1,128)}), f32[8,1,624]{2,1,0:T(1,128)S(1)}, u32[]{:S(2)}, u32[]{:S(2)}) %all-to-all-start) | async-done | bytes 20000 | tf_op jit(solution)/shard_map/all_to_all | solution.py:142
  326.2 7.7 %all_to_all.29 = f32[8,1,624]{2,1,0:T(1,128)S(1)} all-to-all(f32[8,1,624]{2,1,0:T(1,128)S(1)} %all_to_all.23), channel_id=1, replica_groups=mesh['qa'=16,'kb'=8] {'kb'}, dimensions={0} | all-to-all | bytes 39936 | tf_op jit(solution)/shard_map/all_to_all | solution.py:145
  334.0 3.6 all-to-all-start.1
  337.7 32.0 %all-to-all-done.1 = f32[8,624,128]{2,1,0:T(8,128)S(1)} async-done(((f32[8,624,128]{2,1,0:T(8,128)}), f32[8,624,128]{2,1,0:T(8,128)S(1)}, u32[]{:S(2)}, u32[]{:S(2)}) %all-to-all-start.1) | async-done | bytes 2555936 | tf_op jit(solution)/shard_map/all_to_all | solution.py:148
  (151 shorter events, 23.5 us)
Async XLA Ops:
  6.5 36.7 %all-gather.6.cloned.1.call-start = ((), (), s32[]{:S(2)}) async-start(), calls=%async_computation.4 | async-start | bytes 1437696 | tf_op jit(solution)/shard_map/all_gather | solution.py:125
  16.8 74.2 %all-gather.4.cloned.1.call-start = ((), (), s32[]{:S(2)}) async-start(), calls=%async_computation.3 | async-start | bytes 2715648 | tf_op jit(solution)/shard_map/all_gather | solution.py:129
  17.7 121.0 %all-gather.8.cloned.1.call-start = ((), (), s32[]{:S(2)}) async-start(), calls=%async_computation.5 | async-start | bytes 2715648 | tf_op jit(solution)/shard_map/all_gather | solution.py:130
  43.3 97.1 %copy-start = (bf16[4992,128]{1,0:T(8,128)(2,1)S(1)}, bf16[4992,128]{1,0:T(8,128)(2,1)}, u32[]{:S(2)}) copy-start(bf16[4992,128]{1,0:T(8,128)(2,1)} %all-gather.6.cloned.1.call-done) | copy-start | bytes 3833860
  316.4 9.8 %all-to-all-start = ((f32[8,1,624]{2,1,0:T(1,128)}), f32[8,1,624]{2,1,0:T(1,128)S(1)}, u32[]{:S(2)}, u32[]{:S(2)}) async-start(f32[8,1,624]{2,1,0:T(1,128)} %all_to_all.19), calls=%async_computation | async-start | bytes 40960 | tf_op jit(solution)/shard_map/all_to_all | solution.py:142
  334.0 35.7 %all-to-all-start.1 = ((f32[8,624,128]{2,1,0:T(8,128)}), f32[8,624,128]{2,1,0:T(8,128)S(1)}, u32[]{:S(2)}, u32[]{:S(2)}) async-start(f32[8,624,128]{2,1,0:T(8,128)} %bitcast.12), calls=%async_computation.1 | async-start | bytes 5111808 | tf_op jit(solution)/shard_map/all_to_all | solution.py:148
Sparse Core Ops, SparseCore 0:
  16.9 26.3 all-gather.5
  45.4 45.5 all-gather.3
  93.2 45.4 all-gather.7
where the time goes:
time: 380 us; the launch traced here: 378 us
  waiting for transfers between devices  158 us (42%)
  matrix products  81.8 us (22%)
  loops' own time  42.9 us (11%)
  local copies, waits for them, and re-layouts  41 us (11%)
  other arithmetic  24.8 us (7%)
  between operations  13.2 us (3%)
  starting transfers between devices  8.14 us (2%)
  blocking collectives  7.73 us (2%)
    dot_general x9, matrix products, update_group(): jnp.dot(weights.astype(jnp.bfloat16), value_block, preferred_element_type...  57 us
    all_gather x1, waiting for transfers between devices, local(): key_piece = lax.all_gather(key_turned, 'qa', axis=0, tiled=True)  47.8 us
    all_gather x1, waiting for transfers between devices, local(): value_piece = lax.all_gather(value_rows, 'qa', axis=0, tiled=True)  47.7 us
    another operation x1, loops' own time, attend(): return lax.fori_loop(0, key_count, over_keys, running)  42.3 us
    all_to_all x1, waiting for transfers between devices, local(): lax.all_to_all(numerators.reshape(column_devices, tile_rows, head_size),...  32 us
    dynamic_slice x32, local copies, waits for them, and re-layouts, visit(): allowed = pair_table[query_spans[query_index], key_spans[key_index]] > 0  29.8 us
    all_gather x1, waiting for transfers between devices, local(): row_queries = lax.all_gather(query_turned, 'kb', axis=0, tiled=True)  24.8 us
    dot_general x9, matrix products, update_group(): lax.dot_general(query_block, key_block, (((1,), (1,)), ((), ())), preferr...  24.8 us
  transfers between devices with their start and end apart: 5, of which 5 were waited for; matrix products, arithmetic and copies ran while one was open for 0% of the time, Pallas kernels for 0%

commit v1 on v0

v1 whole, which is shorter than its diff:
```python
import functools
import jax
import jax.numpy as jnp
import numpy as np
from jax import lax
from jax.experimental import pallas as pl
from jax.experimental.pallas import tpu as pltpu
from jax.sharding import PartitionSpec as P

HEIGHT = 32
WIDTH = 52
SPANS = 16
TILE = 624
HEAD = 128
PIECE = 80
STARTS = tuple(16 * (i * 34 // 7) for i in range(8))
MESH = pl.DeviceIdType.MESH
BF16 = jnp.bfloat16
F32 = jnp.float32
ROWS = 4 * PIECE
UNROLL = 4
SCALE = float(HEAD ** -0.5)
SCALE2 = float(HEAD ** -0.5 * np.log2(np.e))
LIMIT = 72.0


def coords():
    qa = lax.axis_index("qa")
    kb = lax.axis_index("kb")
    return qa, kb, kb // 2, kb % 2


def turn_table(freq_ref, fo_ref, ho_ref, wo_ref, qa, kb):
    row = lax.broadcasted_iota(jnp.int32, (TILE, HEAD), 0)
    lane = lax.broadcasted_iota(jnp.int32, (TILE, HEAD), 1) % 64
    within = (row + kb * TILE).astype(F32)
    frame = jnp.floor((within + 0.5) * (1.0 / (HEIGHT * WIDTH)))
    line = jnp.floor((within + 0.5) * (1.0 / WIDTH))
    column = within - line * WIDTH + wo_ref[qa].astype(F32)
    line = line - frame * HEIGHT + ho_ref[qa].astype(F32)
    frame = frame + fo_ref[qa].astype(F32)
    angles = jnp.where(lane < 22, frame, jnp.where(lane < 43, line, column)) * freq_ref[...]
    turns = jnp.floor(angles * np.float32(2 / np.pi) + 0.5)
    rest = angles - turns * np.float32(1.5703125)
    rest = rest - turns * np.float32(4.837512969970703125e-4)
    rest = rest - turns * np.float32(7.54978995489188216e-8)
    sq = rest * rest
    sine = rest + rest * sq * (np.float32(-1 / 6) + sq * (np.float32(8.3333333e-3) + sq * (np.float32(-1.98412698e-4) + sq * np.float32(2.7525562e-6))))
    cosine = 1.0 + sq * (np.float32(-0.5) + sq * (np.float32(4.16666667e-2) + sq * (np.float32(-1.38888889e-3) + sq * (np.float32(2.48015873e-5) + sq * np.float32(-2.7557319e-7)))))
    half = jnp.floor(turns * 0.5)
    odd = (turns - 2.0 * half) > 0.5
    flip = (half - 2.0 * jnp.floor(half * 0.5)) > 0.5
    sign = jnp.where(flip, -1.0, 1.0)
    cos_out = jnp.where(odd, -sine, cosine) * sign
    sin_out = jnp.where(odd, cosine, sine) * sign
    full_lane = lax.broadcasted_iota(jnp.int32, (TILE, HEAD), 1)
    return cos_out, jnp.where(full_lane < 64, -sin_out, sin_out)


def turn(rows, cos_out, sin_out):
    x = rows.astype(F32)
    return (x * cos_out + pltpu.roll(x, 64, 1) * sin_out).astype(BF16)


def longest(rows):
    x = rows.astype(F32)
    return jnp.max(jnp.sum(x * x, axis=1, keepdims=True), axis=0, keepdims=True)


def move_kernel(q_ref, k_ref, v_ref, freq_ref, fo_ref, ho_ref, wo_ref, qg, kv, bound,
                qs, q_send, q_recv, z_send, z_recv, s_send, s_recv, kv_send, kv_recv, local_sem):
    qa, kb, z, core = coords()
    step_a = 1 + 3 * core
    step_b = 4 - 3 * core
    a = (qa // step_a) % 4
    b = (qa // step_b) % 4
    primary = (qa // 8) == core

    def at(aa, bb):
        return (aa % 4) * step_a + (bb % 4) * step_b

    barrier = pltpu.get_barrier_semaphore()
    for d in range(1, SPANS):
        pl.semaphore_signal(barrier, inc=1, device_id=((qa + d) % SPANS, kb), device_id_type=MESH)
    for other in ((kb + 2) % 8, (kb + 6) % 8, z * 2 + 1 - core):
        pl.semaphore_signal(barrier, inc=1, device_id=(qa, other), device_id_type=MESH)
    cos_out, sin_out = turn_table(freq_ref, fo_ref, ho_ref, wo_ref, qa, kb)
    qs[...] = turn(q_ref[...], cos_out, sin_out)
    kv[qa, 0] = turn(k_ref[...], cos_out, sin_out)
    kv[qa, 1] = v_ref[...]
    pl.semaphore_wait(barrier, 18)

    def remote(src, dst, send, recv, device):
        return pltpu.make_async_remote_copy(src_ref=src, dst_ref=dst, send_sem=send, recv_sem=recv, device_id=device, device_id_type=MESH)

    q_copies = []
    for i in range(8):
        r = 8 * core + i
        q_copies.append((r, remote(qs.at[pl.ds(STARTS[i], PIECE)], qg.at[z, qa], q_send.at[i], q_recv.at[qa], (r, kb))))
    for r, copy in q_copies:
        @pl.when(r != qa)
        def _():
            copy.start()
    for i in range(8):
        @pl.when(8 * core + i == qa)
        def _():
            own = pltpu.make_async_copy(qs.at[pl.ds(STARTS[i], PIECE)], qg.at[z, qa], local_sem)
            own.start()
            own.wait()

    sends = []
    count = [0]

    def kv_copy(src, part, recv_index, device):
        n = count[0]
        count[0] += 1
        ref = kv.at[src] if part is None else kv.at[src, part]
        copy = remote(ref, ref, kv_send.at[n], kv_recv.at[recv_index], device)
        copy.start()
        sends.append(copy)

    def kv_wait(src, part, recv_index):
        ref = kv.at[src] if part is None else kv.at[src, part]
        remote(ref, ref, kv_send.at[0], kv_recv.at[recv_index], (qa, kb)).wait_recv()

    up_a, down_a = (at(a + 1, b), kb), (at(a - 1, b), kb)
    up_b, down_b = (at(a, b + 1), kb), (at(a, b - 1), kb)
    kv_copy(qa, None, 0, up_a)
    kv_copy(qa, None, 1, down_a)

    def second(item, aa):
        kv_copy(at(aa, b), None, 4 + 4 * item, up_b)
        kv_copy(at(aa, b), None, 5 + 4 * item, down_b)

    second(0, a)

    up_z, down_z, twin = (qa, (kb + 2) % 8), (qa, (kb + 6) % 8), (qa, z * 2 + 1 - core)
    low, high = pl.ds(0, 8), pl.ds(8, 8)
    zm, zp, zo = (z + 3) % 4, (z + 1) % 4, (z + 2) % 4

    def zc(quarter, rows, sem, recv, device):
        ref = qg.at[quarter] if rows is None else qg.at[quarter, rows]
        return remote(ref, ref, sem[0].at[sem[1]], recv[0].at[recv[1]], device)

    @pl.when(primary)
    def _():
        for c in range(SPANS):
            @pl.when(c != qa)
            def _():
                remote(qs.at[pl.ds(0, PIECE)], qg.at[z, c], q_send.at[0], q_recv.at[c], (qa, kb)).wait_recv()
        zc(z, None, (z_send, 0), (z_recv, 0), up_z).start()
        zc(z, None, (z_send, 1), (z_recv, 1), down_z).start()
        zc(z, None, (s_send, 0), (s_recv, 0), twin).start()

    reach = [longest(kv[qa, 0])]

    def look(block):
        reach[0] = jnp.maximum(reach[0], longest(kv[block, 0]))

    kv_wait(at(a - 1, b), None, 0)
    kv_copy(at(a - 1, b), 0, 2, up_a)
    second(1, a - 1)
    kv_wait(at(a + 1, b), None, 1)
    kv_copy(at(a + 1, b), 1, 3, down_a)
    second(2, a + 1)
    look(at(a - 1, b))
    look(at(a + 1, b))

    @pl.when(primary)
    def _():
        zc(zm, None, (z_send, 0), (z_recv, 0), up_z).wait_recv()
        zc(zm, low, (z_send, 2), (z_recv, 2), up_z).start()
        zc(zm, None, (s_send, 1), (s_recv, 1), twin).start()
        zc(zp, None, (z_send, 1), (z_recv, 1), down_z).wait_recv()
        zc(zp, high, (z_send, 3), (z_recv, 3), down_z).start()
        zc(zp, None, (s_send, 2), (s_recv, 2), twin).start()

    kv_wait(at(a + 2, b), 0, 2)
    kv_wait(at(a + 2, b), 1, 3)
    second(3, a + 2)
    look(at(a + 2, b))

    @pl.when(primary)
    def _():
        zc(zo, low, (z_send, 2), (z_recv, 2), up_z).wait_recv()
        zc(zo, high, (z_send, 3), (z_recv, 3), down_z).wait_recv()
        zc(zo, None, (s_send, 3), (s_recv, 3), twin).start()

    items = ((0, a), (1, a - 1), (2, a + 1), (3, a + 2))
    for item, aa in items:
        kv_wait(at(aa, b - 1), None, 4 + 4 * item)
        kv_copy(at(aa, b - 1), 0, 6 + 4 * item, up_b)
        kv_wait(at(aa, b + 1), None, 5 + 4 * item)
        kv_copy(at(aa, b + 1), 1, 7 + 4 * item, down_b)
        look(at(aa, b - 1))
        look(at(aa, b + 1))
    for item, aa in items:
        kv_wait(at(aa, b + 2), 0, 6 + 4 * item)
        kv_wait(at(aa, b + 2), 1, 7 + 4 * item)
        look(at(aa, b + 2))

    @pl.when(jnp.logical_not(primary))
    def _():
        for n, quarter in enumerate((z, zm, zp, zo)):
            zc(quarter, None, (s_send, n), (s_recv, n), twin).wait_recv()

    def stretch(c, best):
        for quarter in range(4):
            best = jnp.maximum(best, longest(qg[quarter, c]))
        return best

    far = lax.fori_loop(0, SPANS, stretch, jnp.zeros((1, 1), F32))
    bound[...] = jnp.broadcast_to(jnp.sqrt(far * reach[0]) * SCALE, bound.shape)

    @pl.when(primary)
    def _():
        zc(z, None, (z_send, 0), (z_recv, 0), up_z).wait_send()
        zc(z, None, (z_send, 1), (z_recv, 1), down_z).wait_send()
        zc(zm, low, (z_send, 2), (z_recv, 2), up_z).wait_send()
        zc(zp, high, (z_send, 3), (z_recv, 3), down_z).wait_send()
        for n, quarter in enumerate((z, zm, zp, zo)):
            zc(quarter, None, (s_send, n), (s_recv, n), twin).wait_send()
    for r, copy in q_copies:
        @pl.when(r != qa)
        def _():
            copy.wait_send()
    for copy in sends:
        copy.wait_send()


def frequencies():
    lead = 1.0 / 10000.0 ** (np.arange(22, dtype=np.float32) / np.float32(22))
    side = 1.0 / 10000.0 ** (np.arange(21, dtype=np.float32) / np.float32(21))
    one = np.concatenate([lead, side, side]).astype(np.float32)
    return jnp.asarray(np.concatenate([one, one])[None])


def move(q, k, v, fo, ho, wo):
    dma = pltpu.SemaphoreType.DMA
    vmem = pl.BlockSpec(memory_space=pltpu.VMEM)
    smem = pl.BlockSpec(memory_space=pltpu.SMEM)
    return pl.pallas_call(
        move_kernel,
        out_shape=[jax.ShapeDtypeStruct((4, SPANS, PIECE, HEAD), BF16), jax.ShapeDtypeStruct((SPANS, 2, TILE, HEAD), BF16),
                   jax.ShapeDtypeStruct((8, HEAD), F32)],
        in_specs=[vmem] * 4 + [smem] * 3,
        out_specs=[vmem, vmem, vmem],
        scratch_shapes=[pltpu.VMEM((TILE, HEAD), BF16), dma((8,)), dma((16,)), dma((4,)), dma((4,)), dma((4,)), dma((4,)), dma((20,)), dma((20,)), dma(())],
        compiler_params=pltpu.CompilerParams(collective_id=0, has_side_effects=True, vmem_limit_bytes=40 << 20),
    )(q, k, v, frequencies(), fo, ho, wo)


def column_to_row(column):
    eye = lax.broadcasted_iota(jnp.int32, column.shape, 0) == lax.broadcasted_iota(jnp.int32, column.shape, 1)
    return jnp.sum(jnp.where(eye, column, 0.0), axis=0, keepdims=True)


def encode(row):
    first = row.astype(BF16).astype(F32)
    second = (row - first).astype(BF16).astype(F32)
    third = (row - first - second).astype(BF16).astype(F32)
    place = lax.broadcasted_iota(jnp.int32, (16, HEAD), 0)
    tile = jnp.where(place == 0, first, jnp.where(place == 1, second, jnp.where(place == 2, third, 0.0)))
    return tile.astype(BF16)


def attend_kernel(table, bound, qg, kv, out, acc, top, cells):
    total = jnp.int32(0)
    for c in range(SPANS):
        for d in range(c + 1):
            cells[total] = c * SPANS + d
            total = total + table[c, d]
    for n in range(UNROLL - 1):
        cells[total + n] = SPANS * SPANS
    acc[...] = jnp.zeros_like(acc)
    ones = jnp.ones((TILE, HEAD), BF16)
    safe = jnp.max(bound[...]) <= LIMIT

    def operands(n):
        code = cells[n]
        c = code // SPANS
        d = code % SPANS
        cc = jnp.minimum(c, SPANS - 1)
        q = jnp.concatenate([qg[i, cc] for i in range(4)], axis=0)
        s = lax.dot_general(q, kv[d, 0], (((1,), (1,)), ((), ())), preferred_element_type=F32)
        return c, s, jnp.concatenate([kv[d, 1], ones], axis=1)

    @pl.when(safe)
    def _():
        @pl.loop(0, (total + UNROLL - 1) // UNROLL)
        def _(step):
            for u in range(UNROLL):
                c, s, v = operands(step * UNROLL + u)
                p = jnp.exp2(s * SCALE2).astype(BF16)
                acc[c] += jnp.dot(p, v, preferred_element_type=F32)

    @pl.when(jnp.logical_not(safe))
    def _():
        top[...] = jnp.full_like(top, -1e30)

        @pl.loop(0, total)
        def _(n):
            c, s, v = operands(n)
            s = s * SCALE
            old = top[c]
            new = jnp.maximum(old, jnp.max(s, axis=1, keepdims=True))
            p = jnp.exp(s - new[:, 0:1]).astype(BF16)
            shrink = jnp.exp(old - new)
            acc[c] = acc[c] * jnp.concatenate([shrink, shrink], axis=1) + jnp.dot(p, v, preferred_element_type=F32)
            top[c] = new

    @pl.loop(0, SPANS)
    def _(c):
        for i in range(4):
            rows = pl.ds(i * PIECE, PIECE)
            sums = acc[c, rows, HEAD:]
            out[i, c, 0:PIECE] = (acc[c, rows, :HEAD] / sums).astype(BF16)
            level = jnp.log(sums) + jnp.where(safe, 0.0, top[c, rows])
            out[i, c, PIECE:] = encode(column_to_row(level))


def attend(table, bound, qg, kv):
    vmem = pl.BlockSpec(memory_space=pltpu.VMEM)
    smem = pl.BlockSpec(memory_space=pltpu.SMEM)
    return pl.pallas_call(
        attend_kernel,
        out_shape=jax.ShapeDtypeStruct((4, SPANS, PIECE + 16, HEAD), BF16),
        in_specs=[smem, vmem, vmem, vmem],
        out_specs=vmem,
        scratch_shapes=[pltpu.VMEM((SPANS + 1, ROWS, 2 * HEAD), F32), pltpu.VMEM((SPANS + 1, ROWS, HEAD), F32), pltpu.SMEM((160,), jnp.int32)],
        compiler_params=pltpu.CompilerParams(vmem_limit_bytes=40 << 20),
    )(table, bound, qg, kv)


def read_rows(block):
    parts = block.astype(F32)
    return parts[0:1] + parts[1:2] + parts[2:3]


def row_to_column(row):
    eye = lax.broadcasted_iota(jnp.int32, (PIECE, HEAD), 0) == lax.broadcasted_iota(jnp.int32, (PIECE, HEAD), 1)
    return jnp.sum(jnp.where(eye, jnp.broadcast_to(row, (PIECE, HEAD)), 0.0), axis=1, keepdims=True)


def merge_kernel(part, out, from_twin, merged, arrived, t_send, t_recv, m_send, m_recv, local_sem):
    qa, kb, z, core = coords()
    home = qa // 8
    twin = (qa, z * 2 + 1 - core)
    mine = pl.ds(8 * core, 8)
    other = pl.ds(8 - 8 * core, 8)
    me_too = jnp.where(home == core, 1, 0)
    slot = qa % 8

    barrier = pltpu.get_barrier_semaphore()
    pl.semaphore_signal(barrier, inc=1, device_id=twin, device_id_type=MESH)
    for i in range(8):
        for zz in range(4):
            @pl.when(jnp.logical_or(8 * core + i != qa, zz * 2 + home != kb))
            def _():
                pl.semaphore_signal(barrier, inc=1, device_id=(8 * core + i, zz * 2 + home), device_id_type=MESH)
    pl.semaphore_wait(barrier, 33 - me_too)

    def remote(src, dst, send, recv, device):
        return pltpu.make_async_remote_copy(src_ref=src, dst_ref=dst, send_sem=send, recv_sem=recv, device_id=device, device_id_type=MESH)

    def swap(n):
        zz = (z + n) % 4
        return remote(part.at[zz, other], from_twin.at[zz], t_send.at[n], t_recv.at[n], twin)

    def give(n, i):
        zz = (z + n) % 4
        return remote(merged.at[zz, i], arrived.at[slot, z], m_send.at[n, i], m_recv.at[slot, z], (8 * core + i, zz * 2 + home))

    order = (2, 1, 3, 0)
    for n in order:
        swap(n).start()
    for n in order:
        zz = (z + n) % 4
        swap(n).wait_recv()
        for i in range(8):
            level_0 = read_rows(part[zz, 8 * core + i, PIECE:])
            level_1 = read_rows(from_twin[zz, i, PIECE:])
            peak = jnp.maximum(level_0, level_1)
            level = peak + jnp.log(jnp.exp(level_0 - peak) + jnp.exp(level_1 - peak))
            share = row_to_column(jnp.exp(level_0 - level))
            x0 = part[zz, 8 * core + i, 0:PIECE].astype(F32)
            x1 = from_twin[zz, i, 0:PIECE].astype(F32)
            merged[zz, i, 0:PIECE] = (x1 + share * (x0 - x1)).astype(BF16)
            merged[zz, i, PIECE:] = encode(level)
            if n == 0:
                @pl.when(8 * core + i != qa)
                def _():
                    give(n, i).start()

                @pl.when(8 * core + i == qa)
                def _():
                    pass
            else:
                give(n, i).start()

    @pl.when(home == core)
    def _():
        keep = pltpu.make_async_copy(merged.at[z, slot], arrived.at[slot, z], local_sem)
        keep.start()
        keep.wait()
    for i in range(8):
        for zz in range(4):
            @pl.when(jnp.logical_or(8 * core + i != qa, zz * 2 + home != kb))
            def _():
                remote(merged.at[0, 0], arrived.at[i, zz], m_send.at[0, 0], m_recv.at[i, zz], (8 * core + i, zz * 2 + home)).wait_recv()
        levels = [read_rows(arrived[i, zz, PIECE:]) for zz in range(4)]
        peak = jnp.maximum(jnp.maximum(levels[0], levels[1]), jnp.maximum(levels[2], levels[3]))
        weights = [jnp.exp(level - peak) for level in levels]
        total = weights[0] + weights[1] + weights[2] + weights[3]
        value = None
        for zz in range(4):
            term = row_to_column(weights[zz] / total) * arrived[i, zz, 0:PIECE].astype(F32)
            value = term if value is None else value + term
        out[STARTS[i]:STARTS[i] + PIECE] = value.astype(BF16)

    for n in order:
        swap(n).wait_send()
        for i in range(8):
            if n == 0:
                @pl.when(8 * core + i != qa)
                def _():
                    give(n, i).wait_send()
            else:
                give(n, i).wait_send()


def merge(part):
    dma = pltpu.SemaphoreType.DMA
    vmem = pl.BlockSpec(memory_space=pltpu.VMEM)
    block = (PIECE + 16, HEAD)
    return pl.pallas_call(
        merge_kernel,
        out_shape=jax.ShapeDtypeStruct((TILE, HEAD), BF16),
        in_specs=[vmem],
        out_specs=vmem,
        scratch_shapes=[pltpu.VMEM((4, 8) + block, BF16), pltpu.VMEM((4, 8) + block, BF16), pltpu.VMEM((8, 4) + block, BF16),
                        dma((4,)), dma((4,)), dma((4, 8)), dma((8, 4)), dma(())],
        compiler_params=pltpu.CompilerParams(collective_id=1, has_side_effects=True, vmem_limit_bytes=40 << 20),
    )(part)


def local(q, k, v, table, fo, ho, wo):
    qg, kv, bound = move(q, k, v, fo, ho, wo)
    return merge(attend(table, bound, qg, kv))


def solution(mesh):
    S = P(("qa", "kb"), None)
    return jax.shard_map(local, mesh=mesh, in_specs=(S, S, S, P(), P(), P(), P()), out_specs=S, check_vma=False)
```

time: 380 us -> 145 us (0.38)
  waiting for transfers between devices: 158 us -> 0 us
  Pallas kernels: 0 us -> 136 us
  matrix products: 81.8 us -> 0 us
  loops' own time: 42.9 us -> 0 us
  local copies, waits for them, and re-layouts: 41 us -> 6.72 us
  other arithmetic: 24.8 us -> 0 us
  between operations: 13.2 us -> 0.04 us
  starting transfers between devices: 8.14 us -> 0 us
  blocking collectives: 7.73 us -> 0 us
    pallas_call x0 -> x3, Pallas kernels: none -> 136 us  [the longest x1 75.9 us: attend(): pl.pallas_call(attend_kernel, out_shape=jax.ShapeDtypeStruct((4, SPANS, P...]
    all_gather x3 -> x0, waiting for transfers between devices: 120 us -> none  [the longest x1 47.8 us: local(): key_piece = lax.all_gather(key_turned, 'qa', axis=0, tiled=True)]
    dot_general x18 -> x0, matrix products: 81.8 us -> none  [the longest x9 57 us: update_group(): jnp.dot(weights.astype(jnp.bfloat16), value_block, preferred_element_type...]
    another operation x17 -> x0, loops' own time: 42.9 us -> none  [the longest x1 42.3 us: attend(): return lax.fori_loop(0, key_count, over_keys, running)]
    all_to_all x2 -> x0, waiting for transfers between devices: 37.2 us -> none  [the longest x1 32 us: local(): lax.all_to_all(numerators.reshape(column_devices, tile_rows, head_size),...]
    dynamic_slice x35 -> x0, local copies, waits for them, and re-layouts: 33.6 us -> none  [the longest x32 29.8 us: visit(): allowed = pair_table[query_spans[query_index], key_spans[key_index]] > 0]
    reduce_sum x11 -> x0, other arithmetic: 19.3 us -> none  [the longest x9 18.4 us: update_group(): totals = totals * shrink + jnp.sum(weights, axis=1)]
    all_to_all x2 -> x0, starting transfers between devices: 8.05 us -> none  [the longest x1 4.42 us: local(): lax.all_to_all(maxima.reshape(column_devices, tile_rows), 'kb', split_axi...]
  transfers between devices with their start and end apart: 5 -> 0, of which waited for: 5 -> 0; matrix products, arithmetic and copies ran while one was open for 0% -> 0% of each run, Pallas kernels for 0% -> 0%
where the time goes in v1:
time: 145 us; the launch traced here: 142 us
  Pallas kernels  136 us (94%)
  local copies, waits for them, and re-layouts  6.72 us (5%)
    pallas_call x1, Pallas kernels, attend(): pl.pallas_call(attend_kernel, out_shape=jax.ShapeDtypeStruct((4, SPANS, P...  75.9 us
    pallas_call x1, Pallas kernels, move(): pl.pallas_call(move_kernel, out_shape=[jax.ShapeDtypeStruct((4, SPANS, PI...  39 us
    pallas_call x1, Pallas kernels, merge(): pl.pallas_call(merge_kernel, out_shape=jax.ShapeDtypeStruct((TILE, HEAD),...  20.8 us
    unnamed x17, local copies, waits for them, and re-layouts  6.72 us

profile of v1, /device:TPU:24, one launch (start us, length us, event | category | flops | bytes accessed | tf_op | source)
XLA Modules:
  0.0 142.4 jit_solution(13656233674641164819)
XLA Ops:
  0.0 0.0 copy-start
  0.0 0.9 copy-done
  0.9 0.0 copy-start.1
  0.9 0.9 copy-done.1
  1.8 0.0 copy-start.2
  1.8 0.9 copy-done.2
  2.7 0.0 copy-start.4
  2.7 0.7 copy-done.4
  3.4 0.0 copy-start.5
  3.4 0.7 copy-done.5
  4.1 0.0 copy-start.6
  4.1 0.7 copy-done.6
  4.7 0.0 copy-start.7
  4.7 0.7 copy-done.7
  5.4 39.0 %shard_map.82 = (bf16[4,16,80,128]{3,2,1,0:T(8,128)(2,1)S(1)}, bf16[16,2,624,128]{3,2,1,0:T(8,128)(2,1)S(1)}, f32[8,128]{1,0:T(8,128)S(1)}) custom-call(bf16[624,128]{1,0:T(8,128)(2,1)S(1)} %copy-done, bf16[624,128]{1,0:T(8,128)(2,1)S(1)} %copy-done.1, bf16[624,128]{1,0:T(8,128)(2,1)S(1)} %copy-done.2, f32[1,128]{1,0:T(1,128)S(1)} %copy-done.7, ...), custom_call_target="tpu_custom_call" | custom-call | tf_op jit(solution)/shard_map/pallas_call | solution.py:242
  44.4 0.0 copy-start.3
  44.4 0.7 copy-done.3
  45.1 75.9 %shard_map.83.part = bf16[4,16,96,128]{3,2,1,0:T(8,128)(2,1)S(1)} custom-call(s32[16,16]{1,0:T(8,128)S(1)} %copy-done.3, f32[8,128]{1,0:T(8,128)S(1)} %get-tuple-element.8.bound, bf16[4,16,80,128]{3,2,1,0:T(8,128)(2,1)S(1)} %get-tuple-element.9.qg, bf16[16,2,624,128]{3,2,1,0:T(8,128)(2,1)S(1)} %get-tuple-element.10.kv), custom_call_target="tpu_custom_call" | custom-call | tf_op jit(solution)/shard_map/pallas_call | solution.py:325
  121.0 20.8 %shard_map.84 = bf16[624,128]{1,0:T(8,128)(2,1)S(1)} custom-call(bf16[4,16,96,128]{3,2,1,0:T(8,128)(2,1)S(1)} %shard_map.83.part), custom_call_target="tpu_custom_call" | custom-call | tf_op jit(solution)/shard_map/pallas_call | solution.py:436
  141.8 0.7 copy.10
Async XLA Ops:
  0.0 0.9 copy-start
  0.9 0.9 copy-start.1
  1.8 0.9 copy-start.2
  2.7 0.7 copy-start.4
  3.4 0.7 copy-start.5
  4.1 0.7 copy-start.6
  4.7 0.7 copy-start.7
  44.4 0.7 copy-start.3

commit v2 on v1

v2 whole, which is shorter than its diff:
```python
import jax
import jax.numpy as jnp
import numpy as np
from jax import lax
from jax.experimental import pallas as pl
from jax.experimental.pallas import tpu as pltpu
from jax.sharding import PartitionSpec as P

HEIGHT = 32
WIDTH = 52
SPANS = 16
TILE = 624
HEAD = 128
PIECE = 80
STARTS = tuple(16 * (i * 34 // 7) for i in range(8))
MESH = pl.DeviceIdType.MESH
BF16 = jnp.bfloat16
F32 = jnp.float32
ROWS = 2 * PIECE
KEYS = 2 * TILE
UNROLL = 4
SCALE = float(HEAD ** -0.5)
SCALE2 = float(HEAD ** -0.5 * np.log2(np.e))
LIMIT = 72.0


def coords():
    qa = lax.axis_index("qa")
    kb = lax.axis_index("kb")
    return qa, kb, kb // 2, kb % 2


def turn_table(freq_ref, fo_ref, ho_ref, wo_ref, qa, kb):
    row = lax.broadcasted_iota(jnp.int32, (TILE, HEAD), 0)
    lane = lax.broadcasted_iota(jnp.int32, (TILE, HEAD), 1) % 64
    within = (row + kb * TILE).astype(F32)
    frame = jnp.floor((within + 0.5) * (1.0 / (HEIGHT * WIDTH)))
    line = jnp.floor((within + 0.5) * (1.0 / WIDTH))
    column = within - line * WIDTH + wo_ref[qa].astype(F32)
    line = line - frame * HEIGHT + ho_ref[qa].astype(F32)
    frame = frame + fo_ref[qa].astype(F32)
    angles = jnp.where(lane < 22, frame, jnp.where(lane < 43, line, column)) * freq_ref[...]
    turns = jnp.floor(angles * np.float32(2 / np.pi) + 0.5)
    rest = angles - turns * np.float32(1.5703125)
    rest = rest - turns * np.float32(4.837512969970703125e-4)
    rest = rest - turns * np.float32(7.54978995489188216e-8)
    sq = rest * rest
    sine = rest + rest * sq * (np.float32(-1 / 6) + sq * (np.float32(8.3333333e-3) + sq * (np.float32(-1.98412698e-4) + sq * np.float32(2.7525562e-6))))
    cosine = 1.0 + sq * (np.float32(-0.5) + sq * (np.float32(4.16666667e-2) + sq * (np.float32(-1.38888889e-3) + sq * (np.float32(2.48015873e-5) + sq * np.float32(-2.7557319e-7)))))
    half = jnp.floor(turns * 0.5)
    odd = (turns - 2.0 * half) > 0.5
    flip = (half - 2.0 * jnp.floor(half * 0.5)) > 0.5
    sign = jnp.where(flip, -1.0, 1.0)
    cos_out = jnp.where(odd, -sine, cosine) * sign
    sin_out = jnp.where(odd, cosine, sine) * sign
    full_lane = lax.broadcasted_iota(jnp.int32, (TILE, HEAD), 1)
    return cos_out, jnp.where(full_lane < 64, -sin_out, sin_out)


def turn(rows, cos_out, sin_out):
    x = rows.astype(F32)
    return (x * cos_out + pltpu.roll(x, 64, 1) * sin_out).astype(BF16)


def longest(rows):
    x = rows.astype(F32)
    return jnp.max(jnp.sum(x * x, axis=1, keepdims=True), axis=0, keepdims=True)


def remote(src, dst, send, recv, device):
    return pltpu.make_async_remote_copy(src_ref=src, dst_ref=dst, send_sem=send, recv_sem=recv, device_id=device, device_id_type=MESH)


def move_kernel(q_in, k_in, v_in, freq_in, fo_in, ho_in, wo_in, qg, kv, bound,
                qs, ks, freq, fo, ho, wo, in_sem, q_send, q_recv, z_send, z_recv, kv_send, kv_recv, t_send, t_recv, local_sem):
    qa, kb, z, core = coords()
    step_a = 1 + 3 * core
    step_b = 4 - 3 * core
    a = (qa // step_a) % 4
    b = (qa // step_b) % 4
    entry = z // 2 == core
    twin = (qa, z * 2 + 1 - core)
    mine = pl.ds(core * TILE, TILE)

    def at(aa, bb):
        return (aa % 4) * step_a + (bb % 4) * step_b

    barrier = pltpu.get_barrier_semaphore()
    loads = [pltpu.make_async_copy(src, dst, in_sem.at[n]) for n, (src, dst) in enumerate((
        (freq_in, freq), (fo_in, fo), (ho_in, ho), (wo_in, wo), (q_in, qs), (k_in, ks), (v_in, kv.at[qa, 1, mine])))]
    for load in loads:
        load.start()
    for d in range(1, SPANS):
        other = (qa + d) % SPANS
        pl.semaphore_signal(barrier, inc=1, device_id=(other, kb), device_id_type=MESH)
        pl.semaphore_signal(barrier, inc=1, device_id=(other, z * 2 + 1 - core), device_id_type=MESH)
    pl.semaphore_signal(barrier, inc=1, device_id=twin, device_id_type=MESH)
    for d in range(1, 4):
        pl.semaphore_signal(barrier, inc=1, device_id=(qa, (kb + 2 * d) % 8), device_id_type=MESH)
    for load in loads:
        load.wait()
    cos_out, sin_out = turn_table(freq, fo, ho, wo, qa, kb)
    qs[...] = turn(qs[...], cos_out, sin_out)
    kv[qa, 0, mine] = turn(ks[...], cos_out, sin_out)
    pl.semaphore_wait(barrier, 34)

    def q_copy(i):
        return remote(qs.at[pl.ds(STARTS[i], PIECE)], qg.at[z % 2, qa], q_send.at[i], q_recv.at[qa], (8 * core + i, z * 2 + z // 2))

    def is_me(i):
        return jnp.logical_and(8 * core + i == qa, entry)

    for i in range(8):
        @pl.when(jnp.logical_not(is_me(i)))
        def _():
            q_copy(i).start()

        @pl.when(is_me(i))
        def _():
            own = pltpu.make_async_copy(qs.at[pl.ds(STARTS[i], PIECE)], qg.at[z % 2, qa], local_sem)
            own.start()
            own.wait()

    sends = []
    count = [0]

    def part_ref(span, part):
        return kv.at[span, part, mine]

    def kv_copy(span, part, device):
        copy = remote(part_ref(span, part), part_ref(span, part), kv_send.at[count[0]], kv_recv.at[span, part], device)
        count[0] += 1
        copy.start()
        sends.append(copy)

    def kv_wait(span, part):
        remote(part_ref(span, part), part_ref(span, part), kv_send.at[0], kv_recv.at[span, part], twin).wait_recv()

    def twin_copy(span, part):
        return remote(part_ref(span, part), part_ref(span, part), t_send.at[span, part], t_recv.at[span, part], twin)

    up_a, down_a = (at(a + 1, b), kb), (at(a - 1, b), kb)
    up_b, down_b = (at(a, b + 1), kb), (at(a, b - 1), kb)
    for part in (1, 0):
        for device in (up_a, down_a, up_b, down_b):
            kv_copy(qa, part, device)
        twin_copy(qa, part).start()

    def z_copy(d):
        return remote(qg.at[z % 2], qg.at[z % 2], z_send.at[d - 1], z_recv.at[z % 2], (qa, (kb + 2 * d) % 8))

    @pl.when(entry)
    def _():
        for c in range(SPANS):
            @pl.when(jnp.logical_or(c != qa, qa // 8 != core))
            def _():
                remote(qs.at[pl.ds(0, PIECE)], qg.at[z % 2, c], q_send.at[0], q_recv.at[c], twin).wait_recv()
        for d in (2, 1, 3):
            z_copy(d).start()

    def arrive(span, part, devices):
        kv_wait(span, part)
        for device in devices:
            kv_copy(span, part, device)
        twin_copy(span, part).start()

    arrive(at(a - 1, b), 1, (up_a, up_b, down_b))
    arrive(at(a + 1, b), 1, (up_b, down_b))
    arrive(at(a, b - 1), 1, (up_b,))
    arrive(at(a, b + 1), 1, ())
    arrive(at(a - 1, b), 0, (up_b, down_b))
    arrive(at(a + 1, b), 0, (down_a, up_b, down_b))
    arrive(at(a, b - 1), 0, ())
    arrive(at(a, b + 1), 0, (down_b,))
    arrive(at(a + 2, b), 1, (up_b, down_b))
    arrive(at(a + 2, b), 0, (up_b, down_b))
    reach = [longest(kv[qa, 0, mine])]

    def look(span):
        reach[0] = jnp.maximum(reach[0], longest(kv[span, 0, mine]))

    for step in (3, 1, 2):
        look(at(a + step, b))
    for step in (3, 1, 2):
        arrive(at(a + step, b - 1), 1, (up_b,))
        arrive(at(a + step, b + 1), 1, ())
        arrive(at(a + step, b - 1), 0, ())
        arrive(at(a + step, b + 1), 0, (down_b,))
        look(at(a + step, b - 1))
        look(at(a + step, b + 1))
    for step in (0, 3, 1, 2):
        arrive(at(a + step, b + 2), 1, ())
        arrive(at(a + step, b + 2), 0, ())
        look(at(a + step, b + 2))

    for span in range(SPANS):
        for part in (1, 0):
            ref = kv.at[span, part, pl.ds((1 - core) * TILE, TILE)]
            remote(ref, ref, t_send.at[0, 0], t_recv.at[span, part], twin).wait_recv()

    for half in range(2):
        @pl.when(jnp.logical_or(jnp.logical_not(entry), half != z % 2))
        def _():
            remote(qg.at[half], qg.at[half], z_send.at[0], z_recv.at[half], twin).wait_recv()

    def other_look(span, best):
        return jnp.maximum(best, longest(kv[span, 0, pl.ds(pl.multiple_of((1 - core) * TILE, 16), TILE)]))

    def stretch(c, best):
        return jnp.maximum(best, jnp.maximum(longest(qg[0, c]), longest(qg[1, c])))

    reach[0] = lax.fori_loop(0, SPANS, other_look, reach[0])
    far = lax.fori_loop(0, SPANS, stretch, jnp.zeros((1, 1), F32))
    bound[...] = jnp.broadcast_to(jnp.sqrt(far * reach[0]) * SCALE, bound.shape)

    @pl.when(entry)
    def _():
        for d in (1, 2, 3):
            z_copy(d).wait_send()
    for i in range(8):
        @pl.when(jnp.logical_not(is_me(i)))
        def _():
            q_copy(i).wait_send()
    for copy in sends:
        copy.wait_send()
    for span in range(SPANS):
        for part in (1, 0):
            twin_copy(span, part).wait_send()


def frequencies():
    lead = 1.0 / 10000.0 ** (np.arange(22, dtype=np.float32) / np.float32(22))
    side = 1.0 / 10000.0 ** (np.arange(21, dtype=np.float32) / np.float32(21))
    one = np.concatenate([lead, side, side]).astype(np.float32)
    return jnp.asarray(np.concatenate([one, one])[None])


def move(q, k, v, fo, ho, wo):
    dma = pltpu.SemaphoreType.DMA
    vmem = pl.BlockSpec(memory_space=pltpu.VMEM)
    anywhere = pl.BlockSpec(memory_space=pl.ANY)
    return pl.pallas_call(
        move_kernel,
        out_shape=[jax.ShapeDtypeStruct((2, SPANS, PIECE, HEAD), BF16), jax.ShapeDtypeStruct((SPANS, 2, KEYS, HEAD), BF16),
                   jax.ShapeDtypeStruct((8, HEAD), F32)],
        in_specs=[anywhere] * 7,
        out_specs=[vmem, vmem, vmem],
        scratch_shapes=[pltpu.VMEM((TILE, HEAD), BF16), pltpu.VMEM((TILE, HEAD), BF16), pltpu.VMEM((1, HEAD), F32),
                        pltpu.SMEM((SPANS,), jnp.int32), pltpu.SMEM((SPANS,), jnp.int32), pltpu.SMEM((SPANS,), jnp.int32),
                        dma((7,)), dma((8,)), dma((16,)), dma((3,)), dma((2,)), dma((30,)), dma((16, 2)), dma((16, 2)), dma((16, 2)), dma(())],
        compiler_params=pltpu.CompilerParams(collective_id=0, has_side_effects=True, vmem_limit_bytes=60 << 20),
    )(q, k, v, frequencies(), fo, ho, wo)


def column_to_row(column):
    eye = lax.broadcasted_iota(jnp.int32, column.shape, 0) == lax.broadcasted_iota(jnp.int32, column.shape, 1)
    return jnp.sum(jnp.where(eye, column, 0.0), axis=0, keepdims=True)


def encode(row):
    first = row.astype(BF16).astype(F32)
    second = (row - first).astype(BF16).astype(F32)
    third = (row - first - second).astype(BF16).astype(F32)
    place = lax.broadcasted_iota(jnp.int32, (16, HEAD), 0)
    tile = jnp.where(place == 0, first, jnp.where(place == 1, second, jnp.where(place == 2, third, 0.0)))
    return tile.astype(BF16)


def attend_kernel(table_in, bound, qg, kv, acc, top, table, cells, sem):
    load = pltpu.make_async_copy(table_in, table, sem)
    load.start()
    acc[...] = jnp.zeros_like(acc)
    ones = jnp.ones((KEYS, HEAD), BF16)
    safe = jnp.max(bound[...]) <= LIMIT
    load.wait()
    total = jnp.int32(0)
    for c in range(SPANS):
        for d in range(c + 1):
            cells[total] = c * SPANS + d
            total = total + table[c, d]
    for n in range(UNROLL - 1):
        cells[total + n] = SPANS * SPANS

    def operands(n):
        code = cells[n]
        c = code // SPANS
        d = code % SPANS
        cc = jnp.minimum(c, SPANS - 1)
        q = jnp.concatenate([qg[0, cc], qg[1, cc]], axis=0)
        s = lax.dot_general(q, kv[d, 0], (((1,), (1,)), ((), ())), preferred_element_type=F32)
        return c, s, jnp.concatenate([kv[d, 1], ones], axis=1)

    @pl.when(safe)
    def _():
        top[...] = jnp.zeros_like(top)

        @pl.loop(0, (total + UNROLL - 1) // UNROLL)
        def _(step):
            for u in range(UNROLL):
                c, s, v = operands(step * UNROLL + u)
                p = jnp.exp2(s * SCALE2).astype(BF16)
                acc[c] += jnp.dot(p, v, preferred_element_type=F32)

    @pl.when(jnp.logical_not(safe))
    def _():
        top[...] = jnp.full_like(top, -1e30)

        @pl.loop(0, total)
        def _(n):
            c, s, v = operands(n)
            s = s * SCALE
            old = top[c]
            new = jnp.maximum(old, jnp.max(s, axis=1, keepdims=True))
            p = jnp.exp(s - new[:, 0:1]).astype(BF16)
            shrink = jnp.exp(old - new)
            acc[c] = acc[c] * jnp.concatenate([shrink, shrink], axis=1) + jnp.dot(p, v, preferred_element_type=F32)
            top[c] = new


def attend(table, bound, qg, kv):
    vmem = pl.BlockSpec(memory_space=pltpu.VMEM)
    return pl.pallas_call(
        attend_kernel,
        out_shape=[jax.ShapeDtypeStruct((SPANS + 1, ROWS, 2 * HEAD), F32), jax.ShapeDtypeStruct((SPANS + 1, ROWS, HEAD), F32)],
        in_specs=[pl.BlockSpec(memory_space=pl.ANY), vmem, vmem, vmem],
        out_specs=[vmem, vmem],
        scratch_shapes=[pltpu.SMEM((SPANS, SPANS), jnp.int32), pltpu.SMEM((160,), jnp.int32), pltpu.SemaphoreType.DMA(())],
        compiler_params=pltpu.CompilerParams(vmem_limit_bytes=60 << 20),
    )(table, bound, qg, kv)


def read_rows(block):
    parts = block.astype(F32)
    return parts[0:1] + parts[1:2] + parts[2:3]


def row_to_column(row):
    eye = lax.broadcasted_iota(jnp.int32, (PIECE, HEAD), 0) == lax.broadcasted_iota(jnp.int32, (PIECE, HEAD), 1)
    return jnp.sum(jnp.where(eye, jnp.broadcast_to(row, (PIECE, HEAD)), 0.0), axis=1, keepdims=True)


def merge_kernel(acc, top, out, part, arrived, m_send, m_recv, local_sem):
    qa, kb, z, core = coords()
    home = qa // 8
    slot = qa % 8
    mine = z // 2

    barrier = pltpu.get_barrier_semaphore()

    def goes(n, c):
        half = (z + n) % 2
        return half, (c, (2 * core + half) * 2 + home)

    def stays(n, c):
        half, device = goes(n, c)
        return jnp.logical_and(c == qa, device[1] == kb)

    for i in range(8):
        for zz in range(4):
            device = (8 * core + i, zz * 2 + mine)
            @pl.when(jnp.logical_or(device[0] != qa, device[1] != kb))
            def _():
                pl.semaphore_signal(barrier, inc=1, device_id=device, device_id_type=MESH)

    for c in range(SPANS):
        for half in range(2):
            rows = pl.ds(half * PIECE, PIECE)
            sums = acc[c, rows, HEAD:]
            part[half, c, 0:PIECE] = (acc[c, rows, :HEAD] / sums).astype(BF16)
            part[half, c, PIECE:] = encode(column_to_row(jnp.log(sums) + top[c, rows]))
    own = jnp.where(jnp.logical_and(home == core, mine == core), 1, 0)
    pl.semaphore_wait(barrier, 32 - own)

    def give(n, c):
        half, device = goes(n, c)
        return remote(part.at[half, c], arrived.at[slot, z], m_send.at[n, c], m_recv.at[slot, z], device)

    for c in range(SPANS):
        for n in range(2):
            @pl.when(jnp.logical_not(stays(n, c)))
            def _():
                give(n, c).start()

            @pl.when(stays(n, c))
            def _():
                keep = pltpu.make_async_copy(part.at[goes(n, c)[0], c], arrived.at[slot, z], local_sem)
                keep.start()
                keep.wait()

    for i in range(8):
        for zz in range(4):
            device = (8 * core + i, zz * 2 + mine)
            @pl.when(jnp.logical_or(device[0] != qa, device[1] != kb))
            def _():
                remote(part.at[0, 0], arrived.at[i, zz], m_send.at[0, 0], m_recv.at[i, zz], device).wait_recv()
    for i in range(8):
        levels = [read_rows(arrived[i, zz, PIECE:]) for zz in range(4)]
        peak = jnp.maximum(jnp.maximum(levels[0], levels[1]), jnp.maximum(levels[2], levels[3]))
        weights = [jnp.exp(level - peak) for level in levels]
        total = weights[0] + weights[1] + weights[2] + weights[3]
        value = None
        for zz in range(4):
            term = row_to_column(weights[zz] / total) * arrived[i, zz, 0:PIECE].astype(F32)
            value = term if value is None else value + term
        out[STARTS[i]:STARTS[i] + PIECE] = value.astype(BF16)

    for c in range(SPANS):
        for n in range(2):
            @pl.when(jnp.logical_not(stays(n, c)))
            def _():
                give(n, c).wait_send()


def merge(acc, top):
    dma = pltpu.SemaphoreType.DMA
    vmem = pl.BlockSpec(memory_space=pltpu.VMEM)
    block = (PIECE + 16, HEAD)
    return pl.pallas_call(
        merge_kernel,
        out_shape=jax.ShapeDtypeStruct((TILE, HEAD), BF16),
        in_specs=[vmem, vmem],
        out_specs=vmem,
        scratch_shapes=[pltpu.VMEM((2, SPANS) + block, BF16), pltpu.VMEM((8, 4) + block, BF16),
                        dma((2, SPANS)), dma((8, 4)), dma(())],
        compiler_params=pltpu.CompilerParams(collective_id=1, has_side_effects=True, vmem_limit_bytes=60 << 20),
    )(acc, top)


def local(q, k, v, table, fo, ho, wo):
    qg, kv, bound = move(q, k, v, fo, ho, wo)
    return merge(*attend(table, bound, qg, kv))


def solution(mesh):
    rows = P(("qa", "kb"), None)
    return jax.shard_map(local, mesh=mesh, in_specs=(rows, rows, rows, P(), P(), P(), P()), out_specs=rows, check_vma=False)
```

time: 145 us -> 148 us (1.021)
  Pallas kernels: 136 us -> 145 us
  local copies, waits for them, and re-layouts: 6.72 us -> 1.59 us
    pallas_call x2, Pallas kernels: 115 us -> 121 us  [the longest x1 74.6 us: attend(): pl.pallas_call(attend_kernel, out_shape=[jax.ShapeDtypeStruct((SPANS + 1,...]
    unnamed x17 -> x1, local copies, waits for them, and re-layouts: 6.72 us -> 1.59 us
    pallas_call x1, Pallas kernels: 20.8 us -> 24.6 us  [merge(): pl.pallas_call(merge_kernel, out_shape=jax.ShapeDtypeStruct((TILE, HEAD),...]
where the time goes in v2:
time: 148 us; the launch traced here: 147 us
  Pallas kernels  145 us (98%)
  local copies, waits for them, and re-layouts  1.59 us (1%)
    pallas_call x1, Pallas kernels, attend(): pl.pallas_call(attend_kernel, out_shape=[jax.ShapeDtypeStruct((SPANS + 1,...  74.6 us
    pallas_call x1, Pallas kernels, move(): pl.pallas_call(move_kernel, out_shape=[jax.ShapeDtypeStruct((2, SPANS, PI...  46 us
    pallas_call x1, Pallas kernels, merge(): pl.pallas_call(merge_kernel, out_shape=jax.ShapeDtypeStruct((TILE, HEAD),...  24.6 us

profile of v2, /device:TPU:24, one launch (start us, length us, event | category | flops | bytes accessed | tf_op | source)
XLA Modules:
  0.0 146.8 jit_solution(13272070651489037511)
XLA Ops:
  0.0 46.0 %shard_map.82 = (bf16[2,16,80,128]{3,2,1,0:T(8,128)(2,1)}, bf16[16,2,1248,128]{3,2,1,0:T(8,128)(2,1)}, f32[8,128]{1,0:T(8,128)}) custom-call(bf16[624,128]{1,0:T(8,128)(2,1)} %q_in.1, bf16[624,128]{1,0:T(8,128)(2,1)} %k_in.1, bf16[624,128]{1,0:T(8,128)(2,1)} %v_in.1, f32[1,128]{1,0:T(1,128)} %constant.2.clone.freq_in, s32[16]{0:T(128)} %fo_in.1, s32[16]{0:T(128)} %ho_in.1, ...), custom_call_target="tpu_custom_call" | custom-call | tf_op jit(solution)/shard_map/pallas_call | solution.py:242
  46.0 74.6 %shard_map.83 = (f32[17,160,256]{2,1,0:T(8,128)}, f32[17,160,128]{2,1,0:T(8,128)}) custom-call(s32[16,16]{1,0:T(8,128)} %table_in.1, f32[8,128]{1,0:T(8,128)} %get-tuple-element.10.bound, bf16[2,16,80,128]{3,2,1,0:T(8,128)(2,1)} %get-tuple-element.11.qg, bf16[16,2,1248,128]{3,2,1,0:T(8,128)(2,1)} %get-tuple-element.12.kv), custom_call_target="tpu_custom_call" | custom-call | tf_op jit(solution)/shard_map/pallas_call | solution.py:322
  120.6 24.6 %shard_map.84 = bf16[624,128]{1,0:T(8,128)(2,1)} custom-call(f32[17,160,256]{2,1,0:T(8,128)} %get-tuple-element.13.acc, f32[17,160,128]{2,1,0:T(8,128)} %get-tuple-element.14.top), custom_call_target="tpu_custom_call" | custom-call | tf_op jit(solution)/shard_map/pallas_call | solution.py:418
  145.2 1.6 %copy.10 = bf16[624,128]{1,0:T(8,128)(2,1)} copy(bf16[624,128]{1,0:T(8,128)(2,1)} %shard_map.84) | data formatting | bytes 319488

commit v3 on v2

v3 whole, which is shorter than its diff:
```python
import jax
import jax.numpy as jnp
import numpy as np
from jax import lax
from jax.experimental import pallas as pl
from jax.experimental.pallas import tpu as pltpu
from jax.sharding import PartitionSpec as P

HEIGHT = 32
WIDTH = 52
SPANS = 16
TILE = 624
HEAD = 128
PIECE = 80
STARTS = tuple(16 * (i * 34 // 7) for i in range(8))
MESH = pl.DeviceIdType.MESH
BF16 = jnp.bfloat16
F32 = jnp.float32
ROWS = 2 * PIECE
KEYS = 2 * TILE
UNROLL = 4
SCALE = float(HEAD ** -0.5)
SCALE2 = float(HEAD ** -0.5 * np.log2(np.e))
LOWEST = 1e-25
HIGHEST = 1e30


def coords():
    qa = lax.axis_index("qa")
    kb = lax.axis_index("kb")
    return qa, kb, kb // 2, kb % 2


def turn_table(freq_ref, numbers, qa, kb):
    row = lax.broadcasted_iota(jnp.int32, (TILE, HEAD), 0)
    lane = lax.broadcasted_iota(jnp.int32, (TILE, HEAD), 1) % 64
    within = (row + kb * TILE).astype(F32)
    frame = jnp.floor((within + 0.5) * (1.0 / (HEIGHT * WIDTH)))
    line = jnp.floor((within + 0.5) * (1.0 / WIDTH))
    column = within - line * WIDTH + numbers[SPANS + 2, qa].astype(F32)
    line = line - frame * HEIGHT + numbers[SPANS + 1, qa].astype(F32)
    frame = frame + numbers[SPANS, qa].astype(F32)
    angles = jnp.where(lane < 22, frame, jnp.where(lane < 43, line, column)) * freq_ref[...]
    turns = jnp.floor(angles * np.float32(2 / np.pi) + 0.5)
    rest = angles - turns * np.float32(1.5703125)
    rest = rest - turns * np.float32(4.837512969970703125e-4)
    rest = rest - turns * np.float32(7.54978995489188216e-8)
    sq = rest * rest
    sine = rest + rest * sq * (np.float32(-1 / 6) + sq * (np.float32(8.3333333e-3) + sq * (np.float32(-1.98412698e-4) + sq * np.float32(2.7525562e-6))))
    cosine = 1.0 + sq * (np.float32(-0.5) + sq * (np.float32(4.16666667e-2) + sq * (np.float32(-1.38888889e-3) + sq * (np.float32(2.48015873e-5) + sq * np.float32(-2.7557319e-7)))))
    half = jnp.floor(turns * 0.5)
    odd = (turns - 2.0 * half) > 0.5
    flip = (half - 2.0 * jnp.floor(half * 0.5)) > 0.5
    sign = jnp.where(flip, -1.0, 1.0)
    cos_out = jnp.where(odd, -sine, cosine) * sign
    sin_out = jnp.where(odd, cosine, sine) * sign
    full_lane = lax.broadcasted_iota(jnp.int32, (TILE, HEAD), 1)
    return cos_out, jnp.where(full_lane < 64, -sin_out, sin_out)


def turn(rows, cos_out, sin_out):
    x = rows.astype(F32)
    return (x * cos_out + pltpu.roll(x, 64, 1) * sin_out).astype(BF16)


NEAR = ((0, 0), (3, 0), (0, 3), (1, 0), (0, 1), (2, 0), (0, 2))
EARLY = 24
FIRST = (1, 1, 1, 1, 1)


def near_order(core):
    return [(jnp.where(core == 0, j, i), jnp.where(core == 0, i, j)) for i, j in NEAR]


def remote(src, dst, send, recv, device):
    return pltpu.make_async_remote_copy(src_ref=src, dst_ref=dst, send_sem=send, recv_sem=recv, device_id=device, device_id_type=MESH)


def move_kernel(rows_in, freq, numbers_in, qg, kv, acc,
                qs, numbers, in_sem, q_send, q_recv, z_send, z_recv, kv_send, kv_recv, t_send, t_recv):
    qa, kb, z, core = coords()
    step_a = 1 + 3 * core
    step_b = 4 - 3 * core
    a = (qa // step_a) % 4
    b = (qa // step_b) % 4
    entry = z // 2 == core
    twin = (qa, z * 2 + 1 - core)
    mine = pl.ds(core * TILE, TILE)

    def at(aa, bb):
        return (aa % 4) * step_a + (bb % 4) * step_b

    barrier = pltpu.get_barrier_semaphore()
    loads = [pltpu.make_async_copy(numbers_in, numbers, in_sem.at[0]),
             pltpu.make_async_copy(rows_in.at[2], kv.at[qa, 1, mine], in_sem.at[1])]
    for load in loads:
        load.start()
    for device in ((at(a + 1, b), kb), (at(a + 3, b), kb), (at(a, b + 1), kb), (at(a, b + 3), kb), twin):
        pl.semaphore_signal(barrier, inc=1, device_id=device, device_id_type=MESH)

    q_home = z * 2 + qa // 8

    @pl.when(entry)
    def _():
        for c in range(SPANS):
            @pl.when(jnp.logical_or(c != qa, q_home != kb))
            def _():
                pl.semaphore_signal(barrier, inc=1, device_id=(c, q_home), device_id_type=MESH)
    for half in range(2):
        @pl.when(2 * core + half != z)
        def _():
            pl.semaphore_signal(barrier, inc=1, device_id=(qa, (2 * core + half) * 2 + core), device_id_type=MESH)
    acc[...] = jnp.zeros_like(acc)
    for load in loads:
        load.wait()
    cos_out, sin_out = turn_table(freq, numbers, qa, kb)
    qs[...] = turn(rows_in[0], cos_out, sin_out)
    kv[qa, 0, mine] = turn(rows_in[1], cos_out, sin_out)
    greeted = 13 + jnp.where(entry, 3, 0) - jnp.where(jnp.logical_and(entry, qa // 8 == core), 1, 0)
    pl.semaphore_wait(barrier, greeted)

    def q_copy(t):
        i = (qa + t) % 8
        rows = pl.ds(pl.multiple_of(16 * (i * 34 // 7), 16), PIECE)
        return rows, remote(qs.at[rows], qg.at[z % 2, qa], q_send, q_recv, (8 * core + i, z * 2 + z // 2))

    to_me = jnp.logical_and(qa // 8 == core, entry)
    for t in range(1, 8):
        q_copy(t)[1].start()

    @pl.when(jnp.logical_not(to_me))
    def _():
        q_copy(0)[1].start()

    @pl.when(to_me)
    def _():
        pltpu.make_async_copy(qs.at[q_copy(0)[0]], qg.at[z % 2, qa], q_recv).start()


    def part_ref(span, part):
        return kv.at[span, part, mine]

    def kv_copy(span, part, device):
        copy = remote(part_ref(span, part), part_ref(span, part), kv_send, kv_recv.at[span, part], device)
        copy.start()

    def kv_wait(span, part):
        remote(part_ref(span, part), part_ref(span, part), kv_send, kv_recv.at[span, part], twin).wait_recv()

    def slot_of(span):
        return span

    def twin_copy(span):
        ref = kv.at[span, :, mine]
        return remote(ref, ref, t_send, t_recv.at[slot_of(span)], twin)

    def twin_wait(span):
        ref = kv.at[span, :, pl.ds((1 - core) * TILE, TILE)]
        remote(ref, ref, t_send, t_recv.at[slot_of(span)], twin).wait_recv()

    up_a, down_a = (at(a + 1, b), kb), (at(a - 1, b), kb)
    up_b, down_b = (at(a, b + 1), kb), (at(a, b - 1), kb)
    for part in (1, 0):
        for device in (up_a, down_a, up_b, down_b):
            kv_copy(qa, part, device)
    twin_copy(qa).start()

    def z_copy(d):
        return remote(qg.at[z % 2], qg.at[z % 2], z_send.at[d - 1], z_recv.at[z % 2], (qa, (kb + 2 * d) % 8))

    @pl.when(entry)
    def _():
        remote(qg.at[z % 2], qg.at[z % 2], q_send, q_recv, twin).wait_recv()
        for d in (2, 1, 3):
            z_copy(d).start()

    def arrive(span, part, devices):
        kv_wait(span, part)
        for device in devices:
            kv_copy(span, part, device)
        if part == 0:
            twin_copy(span).start()

    arrive(at(a - 1, b), 1, (up_a, up_b, down_b))
    arrive(at(a + 1, b), 1, (up_b, down_b))
    arrive(at(a, b - 1), 1, (up_b,))
    arrive(at(a, b + 1), 1, ())
    arrive(at(a - 1, b), 0, (up_b, down_b))
    arrive(at(a + 1, b), 0, (down_a, up_b, down_b))
    arrive(at(a, b - 1), 0, ())
    arrive(at(a, b + 1), 0, (down_b,))
    arrive(at(a + 2, b), 1, (up_b, down_b))
    arrive(at(a + 2, b), 0, (up_b, down_b))
    ones = jnp.ones((KEYS, HEAD), BF16)

    spans = [at(a + i, b + j) for i, j in near_order(core)]
    begins = [jnp.int32(0)]
    for span in spans:
        begins.append(begins[-1] + SPANS - span)

    def cells(n):
        for u in range(UNROLL):
            t = n + u
            d = spans[0]
            c = d + t
            for span, begin in zip(spans[1:], begins[1:]):
                here = t >= begin
                d = jnp.where(here, span, d)
                c = jnp.where(here, span + t - begin, c)
            cc = jnp.minimum(c, SPANS - 1)
            weight = jnp.where(t < begins[-1], numbers[cc, d], 0).astype(F32)
            q = jnp.concatenate([qg[0, cc], qg[1, cc]], axis=0)
            scores = lax.dot_general(q, kv[d, 0], (((1,), (1,)), ((), ())), preferred_element_type=F32)
            p = jnp.exp2(scores * SCALE2).astype(BF16)
            v = jnp.concatenate([kv[d, 1], ones], axis=1)
            acc[cc] += weight * jnp.dot(p, v, preferred_element_type=F32)

    arrive(at(a, b + 2), 1, ())
    arrive(at(a, b + 2), 0, ())
    done = [0]

    def next_cells(n):
        start = done[0]
        done[0] = min(EARLY // UNROLL, start + n)

        @pl.loop(start, done[0])
        def _(step):
            cells(step * UNROLL)

    def events(step, middle, last):
        arrive(at(a + step, b - 1), 1, (up_b,))
        arrive(at(a + step, b + 1), 1, ())
        next_cells(middle)
        arrive(at(a + step, b - 1), 0, ())
        arrive(at(a + step, b + 1), 0, (down_b,))
        next_cells(last)

    events(3, 0, 0)
    for half in range(2):
        @pl.when(jnp.logical_or(jnp.logical_not(entry), half != z % 2))
        def _():
            remote(qg.at[half], qg.at[half], z_send.at[0], z_recv.at[half], twin).wait_recv()
    for i, j in NEAR:
        twin_wait(at(a + i, b + j))
    next_cells(FIRST[0])
    events(1, FIRST[1], FIRST[2])
    events(2, FIRST[3], FIRST[4])
    next_cells(EARLY)
    for step in (3, 1, 2):
        arrive(at(a + step, b + 2), 1, ())
        arrive(at(a + step, b + 2), 0, ())
    for i in (0, 3, 1, 2):
        for j in (0, 3, 1, 2):
            if (i, j) not in NEAR:
                twin_wait(at(a + i, b + j))

    @pl.when(entry)
    def _():
        for d in (1, 2, 3):
            z_copy(d).wait_send()
    @pl.when(to_me)
    def _():
        remote(qg.at[0, pl.ds(0, 7)], qg.at[0, pl.ds(0, 7)], q_send, q_recv, twin).wait_send()

    @pl.when(jnp.logical_not(to_me))
    def _():
        remote(qg.at[0, pl.ds(0, 8)], qg.at[0, pl.ds(0, 8)], q_send, q_recv, twin).wait_send()
    ref = kv.at[pl.ds(0, 15), :, mine]
    remote(ref, ref, kv_send, kv_recv.at[0, 0], twin).wait_send()
    ref = kv.at[:, :, mine]
    remote(ref, ref, t_send, t_recv.at[0], twin).wait_send()


def frequencies():
    lead = 1.0 / 10000.0 ** (np.arange(22, dtype=np.float32) / np.float32(22))
    side = 1.0 / 10000.0 ** (np.arange(21, dtype=np.float32) / np.float32(21))
    one = np.concatenate([lead, side, side]).astype(np.float32)
    return jnp.asarray(np.concatenate([one, one])[None])


def move(rows, numbers):
    dma = pltpu.SemaphoreType.DMA
    vmem = pl.BlockSpec(memory_space=pltpu.VMEM)
    anywhere = pl.BlockSpec(memory_space=pl.ANY)
    return pl.pallas_call(
        move_kernel,
        out_shape=[jax.ShapeDtypeStruct((2, SPANS, PIECE, HEAD), BF16), jax.ShapeDtypeStruct((SPANS, 2, KEYS, HEAD), BF16),
                   jax.ShapeDtypeStruct((SPANS, ROWS, 2 * HEAD), F32)],
        in_specs=[vmem, vmem, anywhere],
        out_specs=[vmem] * 3,
        scratch_shapes=[pltpu.VMEM((TILE, HEAD), BF16), pltpu.SMEM((SPANS + 3, SPANS), jnp.int32),
                        dma((2,)), dma(()), dma(()), dma((3,)), dma((2,)), dma(()), dma((16, 2)), dma(()), dma((16,))],
        compiler_params=pltpu.CompilerParams(collective_id=0, has_side_effects=True, vmem_limit_bytes=24 << 20),
    )(rows, frequencies(), numbers)


def column_to_row(column):
    eye = lax.broadcasted_iota(jnp.int32, column.shape, 0) == lax.broadcasted_iota(jnp.int32, column.shape, 1)
    return jnp.sum(jnp.where(eye, column, 0.0), axis=0, keepdims=True)


def encode(row):
    first = row.astype(BF16).astype(F32)
    second = (row - first).astype(BF16).astype(F32)
    third = (row - first - second).astype(BF16).astype(F32)
    place = lax.broadcasted_iota(jnp.int32, (16, HEAD), 0)
    tile = jnp.where(place == 0, first, jnp.where(place == 1, second, jnp.where(place == 2, third, 0.0)))
    return tile.astype(BF16)


def attend_kernel(table_in, qg, kv, begun, acc, top, table, cells, keep, sem):
    load = pltpu.make_async_copy(table_in, table, sem)
    load.start()
    acc[:SPANS] = begun[...]
    acc[SPANS] = jnp.zeros((ROWS, 2 * HEAD), F32)
    ones = jnp.ones((KEYS, HEAD), BF16)
    qa = lax.axis_index("qa")
    for d in range(SPANS):
        keep[d] = jnp.int32(EARLY)
    begin = jnp.int32(0)
    for i, j in NEAR:
        d = (qa // 4 + i) % 4 * 4 + (qa + j) % 4
        keep[d] = begin
        begin = begin + SPANS - d
    load.wait()

    def gather(skip):
        total = jnp.int32(0)
        for c in range(SPANS):
            for d in range(c + 1):
                cells[total] = c * SPANS + d
                allowed = table[c, d]
                total = total + (jnp.where(keep[d] + (c - d) >= EARLY, allowed, 0) if skip else allowed)
        for n in range(UNROLL - 1):
            cells[total + n] = SPANS * SPANS
        return total

    def operands(n):
        code = cells[n]
        c = code // SPANS
        d = code % SPANS
        cc = jnp.minimum(c, SPANS - 1)
        q = jnp.concatenate([qg[0, cc], qg[1, cc]], axis=0)
        s = lax.dot_general(q, kv[d, 0], (((1,), (1,)), ((), ())), preferred_element_type=F32)
        return c, s, jnp.concatenate([kv[d, 1], ones], axis=1)

    top[...] = jnp.zeros_like(top)
    total = gather(True)

    @pl.loop(0, (total + UNROLL - 1) // UNROLL)
    def _(step):
        for u in range(UNROLL):
            c, s, v = operands(step * UNROLL + u)
            p = jnp.exp2(s * SCALE2).astype(BF16)
            acc[c] += jnp.dot(p, v, preferred_element_type=F32)

    sums = acc[:SPANS, :, HEAD:]
    good = jnp.where(jnp.logical_and(sums >= LOWEST, sums <= HIGHEST), 1.0, 0.0)

    @pl.when(jnp.min(good) < 0.5)
    def _():
        top[...] = jnp.full_like(top, -1e30)
        acc[...] = jnp.zeros_like(acc)
        total = gather(False)

        @pl.loop(0, total)
        def _(n):
            c, s, v = operands(n)
            s = s * SCALE
            old = top[c]
            new = jnp.maximum(old, jnp.max(s, axis=1, keepdims=True))
            p = jnp.exp(s - new[:, 0:1]).astype(BF16)
            shrink = jnp.exp(old - new)
            acc[c] = acc[c] * jnp.concatenate([shrink, shrink], axis=1) + jnp.dot(p, v, preferred_element_type=F32)
            top[c] = new


def attend(table, qg, kv, begun):
    vmem = pl.BlockSpec(memory_space=pltpu.VMEM)
    return pl.pallas_call(
        attend_kernel,
        out_shape=[jax.ShapeDtypeStruct((SPANS + 1, ROWS, 2 * HEAD), F32), jax.ShapeDtypeStruct((SPANS + 1, ROWS, HEAD), F32)],
        in_specs=[pl.BlockSpec(memory_space=pl.ANY), vmem, vmem, vmem],
        out_specs=[vmem, vmem],
        scratch_shapes=[pltpu.SMEM((SPANS + 3, SPANS), jnp.int32), pltpu.SMEM((160,), jnp.int32), pltpu.SMEM((SPANS,), jnp.int32), pltpu.SemaphoreType.DMA(())],
        compiler_params=pltpu.CompilerParams(vmem_limit_bytes=24 << 20),
    )(table, qg, kv, begun)


def read_rows(block):
    parts = block.astype(F32)
    return parts[0:1] + parts[1:2] + parts[2:3]


def row_to_column(row):
    eye = lax.broadcasted_iota(jnp.int32, (PIECE, HEAD), 0) == lax.broadcasted_iota(jnp.int32, (PIECE, HEAD), 1)
    return jnp.sum(jnp.where(eye, jnp.broadcast_to(row, (PIECE, HEAD)), 0.0), axis=1, keepdims=True)


def merge_kernel(acc, top, out, part, arrived, m_send, m_recv):
    qa, kb, z, core = coords()
    home = qa // 8
    slot = qa % 8
    mine = z // 2

    barrier = pltpu.get_barrier_semaphore()

    own = jnp.logical_and(home == core, mine == core)
    for t in range(8):
        for n in range(4):
            device = (8 * core + (qa + t) % 8, (z + n) % 4 * 2 + mine)
            if t or n:
                pl.semaphore_signal(barrier, inc=1, device_id=device, device_id_type=MESH)
            else:
                @pl.when(jnp.logical_not(own))
                def _():
                    pl.semaphore_signal(barrier, inc=1, device_id=device, device_id_type=MESH)

    def finish(t):
        c = (qa + t) % SPANS
        for half in range(2):
            rows = pl.ds(half * PIECE, PIECE)
            sums = acc[c, rows, HEAD:]
            part[half, c, 0:PIECE] = (acc[c, rows, :HEAD] / sums).astype(BF16)
            part[half, c, PIECE:] = encode(column_to_row(jnp.log(sums) + top[c, rows]))

    def give(t, n):
        c = (qa + t) % SPANS
        half = (z + n) % 2
        return half, c, remote(part.at[half, c], arrived.at[slot, z], m_send, m_recv, (c, (2 * core + half) * 2 + home))

    def send(t):
        for n in range(2):
            half, c, copy = give(t, n)
            if t or n:
                copy.start()
            else:
                @pl.when(own)
                def _():
                    pltpu.make_async_copy(part.at[half, c], arrived.at[slot, z], m_recv).start()

                @pl.when(jnp.logical_not(own))
                def _():
                    copy.start()

    for t in range(8):
        finish(t)
    pl.semaphore_wait(barrier, 32 - jnp.where(own, 1, 0))
    for t in range(8):
        send(t)
    for block in range(2):
        for t in range(8 + 4 * block, 12 + 4 * block):
            finish(t)
        for t in range(8 + 4 * block, 12 + 4 * block):
            send(t)

    remote(arrived, arrived, m_send, m_recv, (qa, kb)).wait_recv()
    for i in range(8):
        levels = [read_rows(arrived[i, zz, PIECE:]) for zz in range(4)]
        peak = jnp.maximum(jnp.maximum(levels[0], levels[1]), jnp.maximum(levels[2], levels[3]))
        weights = [jnp.exp(level - peak) for level in levels]
        total = weights[0] + weights[1] + weights[2] + weights[3]
        value = None
        for zz in range(4):
            term = row_to_column(weights[zz] / total) * arrived[i, zz, 0:PIECE].astype(F32)
            value = term if value is None else value + term
        out[STARTS[i]:STARTS[i] + PIECE] = value.astype(BF16)

    every = part.at[:]

    @pl.when(own)
    def _():
        remote(part.at[0, pl.ds(1, 15)], part.at[0, pl.ds(1, 15)], m_send, m_recv, (qa, kb)).wait_send()
        remote(part.at[1], part.at[1], m_send, m_recv, (qa, kb)).wait_send()

    @pl.when(jnp.logical_not(own))
    def _():
        remote(every, every, m_send, m_recv, (qa, kb)).wait_send()


def merge(acc, top):
    dma = pltpu.SemaphoreType.DMA
    vmem = pl.BlockSpec(memory_space=pltpu.VMEM)
    block = (PIECE + 16, HEAD)
    return pl.pallas_call(
        merge_kernel,
        out_shape=jax.ShapeDtypeStruct((TILE, HEAD), BF16),
        in_specs=[vmem, vmem],
        out_specs=vmem,
        scratch_shapes=[pltpu.VMEM((2, SPANS) + block, BF16), pltpu.VMEM((8, 4) + block, BF16),
                        dma(()), dma(())],
        compiler_params=pltpu.CompilerParams(collective_id=1, has_side_effects=True, vmem_limit_bytes=24 << 20),
    )(acc, top)


def local(q, k, v, table, fo, ho, wo):
    rows = jnp.stack([q, k, v])
    numbers = jnp.concatenate([table, fo[None], ho[None], wo[None]])
    qg, kv, begun = move(rows, numbers)
    return merge(*attend(numbers, qg, kv, begun))


def solution(mesh):
    rows = P(("qa", "kb"), None)
    return jax.shard_map(local, mesh=mesh, in_specs=(rows, rows, rows, P(), P(), P(), P()), out_specs=rows, check_vma=False)
```

time: 148 us -> 148 us (level)
  Pallas kernels: 145 us -> 142 us
  other arithmetic: 0 us -> 1.88 us
    pallas_call x1, Pallas kernels: 74.6 us -> 84.6 us  [attend(): pl.pallas_call(attend_kernel, out_shape=[jax.ShapeDtypeStruct((SPANS + 1,...]
    pallas_call x1, Pallas kernels: 46 us -> 37.5 us  [move(): pl.pallas_call(move_kernel, out_shape=[jax.ShapeDtypeStruct((2, SPANS, PI...]
    pallas_call x1, Pallas kernels: 24.6 us -> 20.3 us  [merge(): pl.pallas_call(merge_kernel, out_shape=jax.ShapeDtypeStruct((TILE, HEAD),...]
where the time goes in v3:
time: 148 us; the launch traced here: 146 us
  Pallas kernels  142 us (96%)
  other arithmetic  1.88 us (1%)
    pallas_call x1, Pallas kernels, attend(): pl.pallas_call(attend_kernel, out_shape=[jax.ShapeDtypeStruct((SPANS + 1,...  84.6 us
    pallas_call x1, Pallas kernels, move(): pl.pallas_call(move_kernel, out_shape=[jax.ShapeDtypeStruct((2, SPANS, PI...  37.5 us
    pallas_call x1, Pallas kernels, merge(): pl.pallas_call(merge_kernel, out_shape=jax.ShapeDtypeStruct((TILE, HEAD),...  20.3 us

profile of v3, /device:TPU:24, one launch (start us, length us, event | category | flops | bytes accessed | tf_op | source)
XLA Modules:
  0.0 145.6 jit_solution(13846466280656732955)
XLA Ops:
  0.0 0.8 pad_add_fusion.numbers_in.table_in
  0.8 1.1 pad_maximum_fusion.rows_in
  1.9 0.0 copy-start
  1.9 0.6 copy-done
  2.5 37.5 %shard_map.82 = (bf16[2,16,80,128]{3,2,1,0:T(8,128)(2,1)S(1)}, bf16[16,2,1248,128]{3,2,1,0:T(8,128)(2,1)S(1)}, f32[16,160,256]{2,1,0:T(8,128)S(1)}) custom-call(bf16[3,624,128]{2,1,0:T(8,128)(2,1)S(1)} %pad_maximum_fusion.rows_in, f32[1,128]{1,0:T(1,128)S(1)} %copy-done, s32[19,16]{1,0:T(8,128)S(1)} %pad_add_fusion.numbers_in.table_in), custom_call_target="tpu_custom_call" | custom-call | tf_op jit(solution)/shard_map/pallas_call | solution.py:285
  40.0 84.6 %shard_map.83 = (f32[17,160,256]{2,1,0:T(8,128)S(1)}, f32[17,160,128]{2,1,0:T(8,128)S(1)}) custom-call(s32[19,16]{1,0:T(8,128)S(1)} %pad_add_fusion.numbers_in.table_in, bf16[2,16,80,128]{3,2,1,0:T(8,128)(2,1)S(1)} %get-tuple-element.10.qg, bf16[16,2,1248,128]{3,2,1,0:T(8,128)(2,1)S(1)} %get-tuple-element.11.kv, f32[16,160,256]{2,1,0:T(8,128)S(1)} %get-tuple-element.12.begun), custom_call_target="tpu_custom_call" | custom-call | tf_op jit(solution)/shard_map/pallas_call | solution.py:380
  124.6 20.3 %shard_map.84 = bf16[624,128]{1,0:T(8,128)(2,1)S(1)} custom-call(f32[17,160,256]{2,1,0:T(8,128)S(1)} %get-tuple-element.13.acc, f32[17,160,128]{2,1,0:T(8,128)S(1)} %get-tuple-element.14.top), custom_call_target="tpu_custom_call" | custom-call | tf_op jit(solution)/shard_map/pallas_call | solution.py:485
  144.9 0.7 copy.10
Async XLA Ops:
  1.9 0.7 copy-start
